TPU v7x, 32 devices: a whole 2x2x4 slice. The times are simulated.
32 devices in a mesh: dp: 8 (over z, y), ctx: 4 (over x, core).
Axes of the slice: x: 2, y: 2, z: 4, core: 2. Of those that a mesh axis runs over, the one named last changes fastest.
Arguments:
- tokens: bfloat16 [8, 1024, 1024], P('dp', 'ctx'), may hold values from -6 to 6
- cotangent: bfloat16 [8, 1024, 1024], P('dp', 'ctx'), may hold values from -6 to 6
- expander: bfloat16 [3432448], P(('dp', 'ctx')), may hold values from -0.1875 to 0.1875
- convolver: bfloat16 [8960], P(('dp', 'ctx')), may hold values from -3 to 3
- contractor: bfloat16 [1572864], P(('dp', 'ctx')), may hold values from -0.15625 to 0.15625
- projector: bfloat16 [786432], P(('dp', 'ctx')), may hold values from -0.1875 to 0.1875
- combiner: bfloat16 [524288], P(('dp', 'ctx')), may hold values from -1 to 1
- widener: bfloat16 [4194304], P(('dp', 'ctx')), may hold values from -0.1875 to 0.1875
- narrower: bfloat16 [2097152], P(('dp', 'ctx')), may hold values from -0.125 to 0.125
- norm_gains: bfloat16 [3584], P(('dp', 'ctx')), may hold values from 0.5 to 1.5
- head_rates: float32 [3, 24], replicated, may hold values from -6 to 2
Outputs:
- layer_output: bfloat16 [8, 1024, 1024], P('dp', 'ctx')
- input_gradient: float32 [8, 1024, 1024], P('dp', 'ctx')
- expander_grad: float32 [3432448], P(('dp', 'ctx'))
- convolver_grad: float32 [8960], P(('dp', 'ctx'))
- contractor_grad: float32 [1572864], P(('dp', 'ctx'))
- projector_grad: float32 [786432], P(('dp', 'ctx'))
- combiner_grad: float32 [524288], P(('dp', 'ctx'))
- widener_grad: float32 [4194304], P(('dp', 'ctx'))
- narrower_grad: float32 [2097152], P(('dp', 'ctx'))
- gains_grad: float32 [3584], P(('dp', 'ctx'))
- rates_grad: float32 [3, 24], replicated
All inputs are finite; a program needn't handle non-finite values.
Results may differ from a plain program's by a relative error of at most 0.014.
Values may be sent and summed in bfloat16 or wider, within the bound.
A program may use at most 256 MiB of HBM per device.

v0:
```python
import jax
import jax.numpy as jnp
from jax import lax
from jax.sharding import PartitionSpec as P

D = 1024
MHEADS = 24
MDIM = 64
STATE = 128
KCONV = 4
AHEADS = 8
KVHEADS = 2
ADIM = 64
FF = 2048
SPAN = 128
DINNER = 1536
CONV_CH = 1792
PROJ = 3352


EPSILON = 1e-05
ROPE_BASE = 10000.0


def passed_along(value, axis, steps):
    count = lax.axis_size(axis)
    leading, last = (max(0, -steps), min(count, count - steps))
    return lax.ppermute(value, axis, [(source, source + steps) for source in range(leading, last)])


def entering_2(x, axis, combine, identity):
    size, mine = (lax.axis_size(axis), lax.axis_index(axis))
    everything = jax.tree.map(
        lambda part, kind: lax.all_gather(part.astype(kind), axis), x, (jnp.bfloat16, jnp.bfloat16)
    )
    start = jax.tree.map(
        lambda part, zero: jnp.broadcast_to(jnp.asarray(zero, part.dtype), part.shape), x, identity
    )

    def turn(k, before):
        reached = k < mine
        new = combine(
            before, jax.tree.map(lambda part, own: part[k].astype(own.dtype), everything, x)
        )
        return jax.tree.map(lambda a, b: jnp.where(reached, a, b), new, before)

    return lax.fori_loop(0, size, turn, start)


def entering_3(x, axis, combine, identity):
    size, mine = (lax.axis_size(axis), lax.axis_index(axis))
    everything = jax.tree.map(
        lambda part, kind: lax.all_gather(part.astype(kind), axis),
        x,
        jax.tree.map(lambda a: jnp.bfloat16 if a.dtype == jnp.float32 else a.dtype, x),
    )
    start = jax.tree.map(
        lambda part, zero: jnp.broadcast_to(jnp.asarray(zero, part.dtype), part.shape), x, identity
    )

    def turn(k, before):
        at = size - 1 - k
        reached = at > mine
        new = combine(
            before, jax.tree.map(lambda part, own: part[at].astype(own.dtype), everything, x)
        )
        return jax.tree.map(lambda a, b: jnp.where(reached, a, b), new, before)

    return lax.fori_loop(0, size, turn, start)


def rms_scale(values):
    return lax.rsqrt(jnp.mean(values * values, -1, keepdims=True) + EPSILON)


def rms_back(values, scale, gain, grad):
    scaled = grad * gain
    values_grad = scale * scaled - values * scale**3 * jnp.mean(scaled * values, -1, keepdims=True)
    gain_grad = jnp.sum(grad * values * scale, axis=(0, 1))
    return (values_grad, gain_grad)


def rotate(values, positions):
    half = values.shape[-1] // 2
    freqs = ROPE_BASE ** (-(jnp.arange(half).astype(jnp.float32) * 2.0 / values.shape[-1]))
    angles = positions[:, None] * freqs[None, :]
    cosine = jnp.cos(angles)[:, None, :]
    sine = jnp.sin(angles)[:, None, :]
    first = values[..., :half]
    second = values[..., half:]
    return jnp.concatenate([first * cosine - second * sine, second * cosine + first * sine], -1)


def span_step(state, block):
    inputs, b_proj, c_proj, step_size, log_decay = block
    cumul = jnp.cumsum(log_decay, axis=1)
    count = cumul.shape[1]
    lower = jnp.arange(count)[:, None] >= jnp.arange(count)[None, :]
    gaps = cumul[:, :, None, :] - cumul[:, None, :, :]
    decays = jnp.exp(jnp.where(lower[None, :, :, None], gaps, -jnp.inf))
    intersection = jnp.einsum("btn,bsn->bts", c_proj, b_proj, precision=lax.Precision.HIGHEST)
    mixing = intersection[..., None] * decays * step_size[:, None, :, :]
    within = jnp.einsum("btsh,bshp->bthp", mixing, inputs, precision=lax.Precision.HIGHEST)
    carried = jnp.exp(cumul)[..., None] * jnp.einsum(
        "btn,bhpn->bthp", c_proj, state, precision=lax.Precision.HIGHEST
    )
    tail = jnp.exp(cumul[:, -1:, :] - cumul) * step_size
    new_state = jnp.exp(cumul[:, -1, :])[:, :, None, None] * state + jnp.einsum(
        "bsh,bsn,bshp->bhpn", tail, b_proj, inputs, precision=lax.Precision.HIGHEST
    )
    return (new_state, within + carried)


def run_spans(inputs, b_proj, c_proj, step_size, log_decay, state):
    batch, length = (inputs.shape[0], inputs.shape[1])
    count = length // SPAN

    def split(values):
        return jnp.moveaxis(values.reshape((batch, count, SPAN) + values.shape[2:]), 1, 0)

    final, outputs = lax.scan(
        jax.checkpoint(span_step),
        state,
        (split(inputs), split(b_proj), split(c_proj), split(step_size), split(log_decay)),
    )
    outputs = jnp.moveaxis(outputs, 0, 1).reshape(batch, length, MHEADS, MDIM)
    return (outputs, final)


def prepare(extended, conv_full, raw_step, head_rates):
    length = extended.shape[1] - (KCONV - 1)
    mixed = conv_full[KCONV]
    for offset in range(KCONV):
        mixed = mixed + conv_full[offset] * extended[:, offset : offset + length]
    activated = jax.nn.silu(mixed)
    inputs = activated[..., :DINNER].reshape(activated.shape[0], length, MHEADS, MDIM)
    b_proj = activated[..., DINNER : DINNER + STATE]
    c_proj = activated[..., DINNER + STATE :]
    step_size = jax.nn.softplus(raw_step + head_rates[0])
    log_decay = -step_size * jnp.exp(head_rates[1])
    return (inputs, b_proj, c_proj, step_size, log_decay)


def mixer(extended, conv_full, raw_step, head_rates, state):
    inputs, b_proj, c_proj, step_size, log_decay = prepare(
        extended, conv_full, raw_step, head_rates
    )
    outputs, final = run_spans(inputs, b_proj, c_proj, step_size, log_decay, state)
    return (outputs + head_rates[2][:, None] * inputs, final)


def combine_states(earlier, later):
    return (earlier[0] * later[0], later[0][:, :, None, None] * earlier[1] + later[1])


def shaped(pieces):
    return (
        pieces[0].reshape(D, PROJ),
        pieces[1].reshape(KCONV + 1, CONV_CH),
        pieces[2].reshape(DINNER, D),
        pieces[3].reshape(D, (AHEADS + 2 * KVHEADS) * ADIM),
        pieces[4].reshape(AHEADS * ADIM, D),
        pieces[5].reshape(D, 2 * FF),
        pieces[6].reshape(FF, D),
        pieces[7],
    )


def masked_scores(grouped, key_all, causal):
    raw_scores = jnp.einsum(
        "btkgd,bskd->bkgts", grouped, key_all, preferred_element_type=jnp.float32
    ) * ADIM ** (-0.5)
    return jnp.where(causal, raw_scores, -jnp.inf)


def project(left, right):
    return jnp.einsum("btd,df->btf", left, right, preferred_element_type=jnp.float32)


def project_back(left, right):
    return jnp.einsum("btf,df->btd", left, right, preferred_element_type=jnp.float32)


def outer_sum(left, right):
    return jnp.einsum("btd,btf->df", left, right, preferred_element_type=jnp.float32)


def local(
    tokens,
    cotangent,
    expander,
    convolver,
    contractor,
    projector,
    combiner,
    widener,
    narrower,
    norm_gains,
    head_rates,
):
    flat_shards = (
        expander,
        convolver,
        contractor,
        projector,
        combiner,
        widener,
        narrower,
        norm_gains,
    )
    weights = shaped(
        (
            lax.all_gather(flat_shards[0], ("dp", "ctx"), axis=0, tiled=True),
            lax.all_gather(flat_shards[1], ("dp", "ctx"), axis=0, tiled=True),
            lax.all_gather(flat_shards[2], ("dp", "ctx"), axis=0, tiled=True),
            lax.all_gather(flat_shards[3], ("dp", "ctx"), axis=0, tiled=True),
            lax.all_gather(flat_shards[4], ("dp", "ctx"), axis=0, tiled=True),
            lax.all_gather(flat_shards[5], ("dp", "ctx"), axis=0, tiled=True),
            lax.all_gather(flat_shards[6], ("dp", "ctx"), axis=0, tiled=True),
            lax.all_gather(flat_shards[7], ("dp", "ctx"), axis=0, tiled=True),
        )
    )
    w_expand, w_conv, w_contract, w_project, w_combine, w_widen, w_narrow, gain_all = weights
    gains = gain_all.astype(jnp.float32)
    first_gain = gains[:D]
    second_gain = gains[D : 2 * D]
    mixer_gain = gains[2 * D :]
    batch, rows = (tokens.shape[0], tokens.shape[1])
    ctx_count = lax.axis_size("ctx")
    here = lax.axis_index("ctx")
    groups = AHEADS // KVHEADS
    stream = tokens.astype(jnp.float32)
    first_scale = rms_scale(stream)
    normed = (stream * first_scale * first_gain).astype(jnp.bfloat16)
    expanded = project(normed, w_expand)
    gate_branch = expanded[..., :DINNER]
    conv_input = expanded[..., DINNER : DINNER + CONV_CH].astype(jnp.bfloat16)
    raw_step = expanded[..., DINNER + CONV_CH :]
    edge = passed_along(conv_input[:, rows - (KCONV - 1) :], "ctx", 1)
    extended = jnp.concatenate([edge, conv_input], 1).astype(jnp.float32)
    conv_full = w_conv.astype(jnp.float32)
    inputs, b_proj, c_proj, step_size, log_decay = prepare(
        extended, conv_full, raw_step, head_rates
    )
    zero_state = jnp.zeros((batch, MHEADS, MDIM, STATE), jnp.float32)
    local_out, local_state = run_spans(inputs, b_proj, c_proj, step_size, log_decay, zero_state)
    cumul = jnp.cumsum(log_decay, axis=1)
    device_decay = jnp.exp(cumul[:, -1, :])
    identity = (jnp.ones_like(device_decay), jnp.zeros_like(local_state))
    prefix = entering_2((device_decay, local_state), "ctx", combine_states, identity)
    entering = prefix[1]
    carried = jnp.exp(cumul)[..., None] * jnp.einsum(
        "btn,bhpn->bthp", c_proj, entering, precision=lax.Precision.HIGHEST
    )
    scanned = local_out + carried + head_rates[2][:, None] * inputs
    scanned_flat = scanned.reshape(batch, rows, DINNER)
    gate_sig = jax.nn.sigmoid(gate_branch)
    gate_act = gate_branch * gate_sig
    gated = scanned_flat * gate_act
    gated_scale = rms_scale(gated)
    gated_norm = (gated * gated_scale * mixer_gain).astype(jnp.bfloat16)
    mixer_branch = project(gated_norm, w_contract)
    projected = project(normed, w_project)
    query_pos = here * rows + jnp.arange(rows)
    positions = query_pos.astype(jnp.float32)
    queries = rotate(
        projected[..., : AHEADS * ADIM].reshape(batch, rows, AHEADS, ADIM), positions
    ).astype(jnp.bfloat16)
    keys = rotate(
        projected[..., AHEADS * ADIM : (AHEADS + KVHEADS) * ADIM].reshape(
            batch, rows, KVHEADS, ADIM
        ),
        positions,
    ).astype(jnp.bfloat16)
    values = (
        projected[..., (AHEADS + KVHEADS) * ADIM :]
        .reshape(batch, rows, KVHEADS, ADIM)
        .astype(jnp.bfloat16)
    )
    key_all, value_all = (
        lax.all_gather(keys, "ctx", axis=1, tiled=True),
        lax.all_gather(values, "ctx", axis=1, tiled=True),
    )
    key_pos = jnp.arange(rows * ctx_count)
    causal = key_pos[None, :] <= query_pos[:, None]
    grouped = queries.reshape(batch, rows, KVHEADS, groups, ADIM)
    scores = masked_scores(grouped, key_all, causal)
    maxima = jnp.max(scores, -1, keepdims=True)
    expos = jnp.exp(scores - maxima)
    totals = jnp.sum(expos, -1, keepdims=True)
    log_total = maxima + jnp.log(totals)
    probs = (expos / totals).astype(jnp.bfloat16)
    attended = jnp.einsum("bkgts,bskd->btkgd", probs, value_all, preferred_element_type=jnp.float32)
    attended = attended.reshape(batch, rows, AHEADS * ADIM).astype(jnp.bfloat16)
    attention_branch = project(attended, w_combine)
    middle = stream + mixer_branch + attention_branch
    second_scale = rms_scale(middle)
    second = (middle * second_scale * second_gain).astype(jnp.bfloat16)
    widened = project(second, w_widen)
    gate_value = widened[..., :FF]
    up_value = widened[..., FF:]
    feed_sig = jax.nn.sigmoid(gate_value)
    activated = (gate_value * feed_sig * up_value).astype(jnp.bfloat16)
    layer_output = (middle + project(activated, w_narrow)).astype(jnp.bfloat16)
    w_expand, w_conv, w_contract, w_project, w_combine, w_widen, w_narrow, gain_all = weights
    outer_grad = cotangent.astype(jnp.float32)
    narrow_grad = outer_sum(activated, cotangent)
    act_grad = project_back(cotangent, w_narrow)
    gate_grad = act_grad * up_value * feed_sig * (1.0 + gate_value * (1.0 - feed_sig))
    up_grad = act_grad * gate_value * feed_sig
    widened_grad = jnp.concatenate([gate_grad, up_grad], -1).astype(jnp.bfloat16)
    widen_grad = outer_sum(second, widened_grad)
    second_grad = project_back(widened_grad, w_widen)
    middle_part, second_gain_grad = rms_back(middle, second_scale, second_gain, second_grad)
    middle_grad = outer_grad + middle_part
    branch_grad = middle_grad.astype(jnp.bfloat16)
    combine_grad = outer_sum(attended, branch_grad)
    attended_grad = project_back(branch_grad, w_combine).astype(jnp.bfloat16)
    attended_grad = attended_grad.reshape(batch, rows, KVHEADS, groups, ADIM)
    scores = masked_scores(grouped, key_all, causal)
    float_probs = jnp.exp(scores - log_total)
    value_part = jnp.einsum(
        "bkgts,btkgd->bskd",
        float_probs.astype(jnp.bfloat16),
        attended_grad,
        preferred_element_type=jnp.float32,
    )
    probs_grad = jnp.einsum(
        "btkgd,bskd->bkgts", attended_grad, value_all, preferred_element_type=jnp.float32
    )
    centre = jnp.sum(probs_grad * float_probs, -1, keepdims=True)
    scores_grad = (float_probs * (probs_grad - centre)).astype(jnp.bfloat16)
    query_grad = ADIM ** (-0.5) * jnp.einsum(
        "bkgts,bskd->btkgd", scores_grad, key_all, preferred_element_type=jnp.float32
    )
    key_part = ADIM ** (-0.5) * jnp.einsum(
        "bkgts,btkgd->bskd", scores_grad, grouped, preferred_element_type=jnp.float32
    )
    key_sum, value_sum = (
        lax.psum_scatter(
            key_part.astype(jnp.bfloat16), "ctx", scatter_dimension=1, tiled=True
        ).astype(jnp.float32),
        lax.psum_scatter(
            value_part.astype(jnp.bfloat16), "ctx", scatter_dimension=1, tiled=True
        ).astype(jnp.float32),
    )
    query_grad = rotate(query_grad.reshape(batch, rows, AHEADS, ADIM), -positions)
    key_sum = rotate(key_sum, -positions)
    projected_grad = jnp.concatenate(
        [
            query_grad.reshape(batch, rows, AHEADS * ADIM),
            key_sum.reshape(batch, rows, KVHEADS * ADIM),
            value_sum.reshape(batch, rows, KVHEADS * ADIM),
        ],
        -1,
    ).astype(jnp.bfloat16)
    project_grad = outer_sum(normed, projected_grad)
    contract_grad = outer_sum(gated_norm, branch_grad)
    gated_norm_grad = project_back(branch_grad, w_contract)
    gated_grad, mixer_gain_grad = rms_back(gated, gated_scale, mixer_gain, gated_norm_grad)
    scanned_grad = (gated_grad * gate_act).reshape(batch, rows, MHEADS, MDIM)
    gate_branch_grad = gated_grad * scanned_flat * gate_sig * (1.0 + gate_branch * (1.0 - gate_sig))
    outgoing = jnp.einsum(
        "bth,bthp,btn->bhpn", jnp.exp(cumul), scanned_grad, c_proj, precision=lax.Precision.HIGHEST
    )
    suffix = entering_3((device_decay, outgoing), "ctx", combine_states, identity)
    leaving_grad = suffix[1]
    primal_out, pullback = jax.vjp(mixer, extended, conv_full, raw_step, head_rates, entering)
    extended_grad, conv_grad, step_grad, rates_local, entering_grad = pullback(
        (scanned_grad, leaving_grad)
    )
    returned = passed_along(extended_grad[:, : KCONV - 1], "ctx", -1)
    conv_input_grad = extended_grad[:, KCONV - 1 :]
    conv_input_grad = jnp.concatenate(
        [
            conv_input_grad[:, : rows - (KCONV - 1)],
            conv_input_grad[:, rows - (KCONV - 1) :] + returned,
        ],
        1,
    )
    expanded_grad = jnp.concatenate([gate_branch_grad, conv_input_grad, step_grad], -1).astype(
        jnp.bfloat16
    )
    expand_grad = outer_sum(normed, expanded_grad)
    normed_grad = project_back(expanded_grad, w_expand) + project_back(projected_grad, w_project)
    input_part, first_gain_grad = rms_back(stream, first_scale, first_gain, normed_grad)
    input_gradient = middle_grad + input_part
    gains_local = jnp.concatenate([first_gain_grad, second_gain_grad, mixer_gain_grad], 0)
    rates_total = lax.psum(rates_local, ("dp", "ctx"))
    local_grads = (
        expand_grad.reshape(-1),
        conv_grad.reshape(-1),
        contract_grad.reshape(-1),
        project_grad.reshape(-1),
        combine_grad.reshape(-1),
        widen_grad.reshape(-1),
        narrow_grad.reshape(-1),
        gains_local,
    )
    g0, g1, g2, g3, g4, g5, g6, g7 = local_grads
    owned = (
        lax.psum_scatter(g0, ("dp", "ctx"), scatter_dimension=0, tiled=True),
        lax.psum_scatter(g1, ("dp", "ctx"), scatter_dimension=0, tiled=True),
        lax.psum_scatter(g2, ("dp", "ctx"), scatter_dimension=0, tiled=True),
        lax.psum_scatter(g3, ("dp", "ctx"), scatter_dimension=0, tiled=True),
        lax.psum_scatter(g4, ("dp", "ctx"), scatter_dimension=0, tiled=True),
        lax.psum_scatter(g5, ("dp", "ctx"), scatter_dimension=0, tiled=True),
        lax.psum_scatter(g6, ("dp", "ctx"), scatter_dimension=0, tiled=True),
        lax.psum_scatter(g7, ("dp", "ctx"), scatter_dimension=0, tiled=True),
    )
    return (
        layer_output,
        input_gradient,
        owned[0],
        owned[1],
        owned[2],
        owned[3],
        owned[4],
        owned[5],
        owned[6],
        owned[7],
        rates_total,
    )


def solution(mesh):
    return jax.shard_map(
        local,
        mesh=mesh,
        in_specs=(
            P("dp", "ctx", None),
            P("dp", "ctx", None),
            P(("dp", "ctx")),
            P(("dp", "ctx")),
            P(("dp", "ctx")),
            P(("dp", "ctx")),
            P(("dp", "ctx")),
            P(("dp", "ctx")),
            P(("dp", "ctx")),
            P(("dp", "ctx")),
            P(),
        ),
        out_specs=(
            P("dp", "ctx", None),
            P("dp", "ctx", None),
            P(("dp", "ctx")),
            P(("dp", "ctx")),
            P(("dp", "ctx")),
            P(("dp", "ctx")),
            P(("dp", "ctx")),
            P(("dp", "ctx")),
            P(("dp", "ctx")),
            P(("dp", "ctx")),
            P(),
        ),
        check_vma=False,
    )
```

profile of v0, /device:TPU:0, one launch (start us, length us, event | category | flops | bytes accessed | tf_op | source)
XLA Modules:
  0.0 1517.6 jit_solution(8826896707779219665)
XLA Ops:
  14.8 43.0 %all-reduce.29 = (bf16[3584]{0:T(1024)(128)(2,1)S(1)}, bf16[8960]{0:T(1024)(128)(2,1)S(1)}) all-reduce(bf16[3584]{0:T(1024)(128)(2,1)S(1)} %dynamic-update-slice, bf16[8960]{0:T(1024)(128)(2,1)S(1)} %dynamic-update-slice.1), channel_id=1, replica_groups=mesh['dp'=8,'ctx'=4] {'dp','ctx'}, use_global_device_ids=true, to_apply=%add.17 | all-reduce | flops 12544 | bytes 50176
  57.9 58.8 %all-gather.26.cloned.1.call-done = bf16[32,1,107264]{2,1,0:T(2,128)(2,1)} async-done(((bf16[1,1,107264]{2,1,0:T(2,128)(2,1)}), bf16[32,1,107264]{2,1,0:T(2,128)(2,1)}) %all-gather.26.cloned.1.call-update) | async-done | bytes 6864912 | tf_op jit(solution)/shard_map/all_gather | solution.py:213
  116.7 103.1 %reduce.70 = bf16[32,107264]{1,0:T(8,128)(2,1)} reduce(bf16[32,1,107264]{2,1,0:T(2,128)(2,1)} %all-gather.26.cloned.1.call-done, bf16[]{:T(256)} %constant.297), dimensions={1}, to_apply=%all-gather.2.reduce_sub_computation | reduce | bytes 13729794 | tf_op jit(solution)/shard_map/all_gather | solution.py:213
  219.8 15.6 %reshape.1488 = bf16[1024,3352]{1,0:T(8,128)(2,1)} reshape(bf16[32,107264]{1,0:T(8,128)(2,1)} %reduce.70) | data formatting | bytes 13729792 | tf_op jit(solution)/shard_map/reshape | solution.py:158
  235.4 5.2 fusion.226
  245.7 14.4 fusion.219
  269.1 54.4 %while.81 = (s32[]{:T(128)}, f32[1,24,64,128]{3,2,1,0:T(8,128)S(1)}, f32[2,1,128,24,64]{2,0,4,3,1:T(2,128)}, f32[2,1,128,24]{3,2,1,0:T(8,128)}, f32[2,1,128,24]{...) while((s32[]{:T(128)}, ...), condition=%wide.region_3.4_spmd.clone, body=%wide.region_1.3_spmd.clone.sunk | while | flops 934497280 | bytes 8564755 | solution.py:121
  277.3 19.0 %dynamic_update_slice.72 = f32[2,1,128,24,64]{2,0,4,3,1:T(2,128)} dynamic-update-slice(f32[2,1,128,24,64]{2,0,4,3,1:T(2,128)} %get-tuple-element.1435, f32[1,1,128,24,64]{2,0,4,3,1:T(1,128)S(1)} %bitcast.730, s32[]{:T(128)S(6)} %copy.636, s32[]{:T(128)} %constant.213.clone.1..sunk.1, s32[]{:T(128)} %constant.213.clone.1..sunk.1, s32[]{:T(128)} %constant.213.clone.1..sunk.1, ...) | dynamic-update-slice | bytes 1572868 | tf_op jit(solution)/shard_map/while/body/jit(dynamic_update_index_in_dim)/dynamic_update_slice | solution.py:121
  304.5 19.0 %dynamic_update_slice.72 = f32[2,1,128,24,64]{2,0,4,3,1:T(2,128)} dynamic-update-slice(f32[2,1,128,24,64]{2,0,4,3,1:T(2,128)} %get-tuple-element.1435, f32[1,1,128,24,64]{2,0,4,3,1:T(1,128)S(1)} %bitcast.730, s32[]{:T(128)S(6)} %copy.636, s32[]{:T(128)} %constant.213.clone.1..sunk.1, s32[]{:T(128)} %constant.213.clone.1..sunk.1, s32[]{:T(128)} %constant.213.clone.1..sunk.1, ...) | dynamic-update-slice | bytes 1572868 | tf_op jit(solution)/shard_map/while/body/jit(dynamic_update_index_in_dim)/dynamic_update_slice | solution.py:121
  343.9 7.0 all_gather.57
  350.9 6.1 all_gather.56
  365.9 5.8 reshape.1499
  371.7 7.3 reshape.1510
  394.0 5.3 all_gather.51
  402.7 4.8 copy.430
  410.9 7.3 while.82
  418.2 4.5 multiply_add_fusion.1
  426.3 4.9 copy.433
  431.2 5.5 multiply_reduce_fusion.9
  441.8 11.0 all-gather.18.cloned.1.call-done
  452.8 13.6 reshape.1508
  466.4 6.2 convolution_bitcast_fusion.9
  486.5 5.5 fusion.110
  498.5 8.7 multiply_reduce_fusion.7
  507.2 5.5 fusion.146
  512.8 4.7 fusion.166
  517.5 4.8 multiply_reduce_fusion.6
  522.4 4.8 copy.441
  530.9 8.5 while.79
  539.4 6.0 copy.447
  548.7 4.2 copy.534
  554.2 5.4 copy.537
  562.0 7.0 copy.536
  575.1 4.4 reshape.1521
  579.6 7.4 while.83
  591.5 123.5 %while.80 = (s32[]{:T(128)}, f32[1,24,64,128]{3,2,1,0:T(8,128)S(1)}, f32[2,1,128,24,64]{2,0,1,4,3:T(2,128)}, f32[2,1,128,128]{3,2,0,1:T(8,128)}, f32[2,1,128,128...) while((s32[]{:T(128)}, ...), condition=%wide.region_29.30_spmd, body=%wide.region_19.29_spmd.sunk | while | flops 2199523328 | bytes 45209780 | solution.py:121
  609.1 4.6 fusion.316
  634.3 19.0 %dynamic_update_slice.71 = f32[2,1,128,24,64]{2,0,1,4,3:T(2,128)} dynamic-update-slice(f32[2,1,128,24,64]{2,0,1,4,3:T(2,128)} %get-tuple-element.1549, f32[1,1,128,24,64]{2,0,1,4,3:T(1,128)} %bitcast.738, s32[]{:T(128)S(6)} %sub.415, s32[]{:T(128)} %constant.213.clone.1..sunk, s32[]{:T(128)} %constant.213.clone.1..sunk, s32[]{:T(128)} %constant.213.clone.1..sunk, s32[]{:T(128)} %constant.213.clone.1..sunk) | dynamic-update-slice | bytes 1572868 | tf_op jit(solution)/shard_map/transpose(jvp())/while/body/jit(dynamic_update_index_in_dim)/dynamic_update_slice | solution.py:121
  670.6 4.6 fusion.316
  695.8 19.0 %dynamic_update_slice.71 = f32[2,1,128,24,64]{2,0,1,4,3:T(2,128)} dynamic-update-slice(f32[2,1,128,24,64]{2,0,1,4,3:T(2,128)} %get-tuple-element.1549, f32[1,1,128,24,64]{2,0,1,4,3:T(1,128)} %bitcast.738, s32[]{:T(128)S(6)} %sub.415, s32[]{:T(128)} %constant.213.clone.1..sunk, s32[]{:T(128)} %constant.213.clone.1..sunk, s32[]{:T(128)} %constant.213.clone.1..sunk, s32[]{:T(128)} %constant.213.clone.1..sunk) | dynamic-update-slice | bytes 1572868 | tf_op jit(solution)/shard_map/transpose(jvp())/while/body/jit(dynamic_update_index_in_dim)/dynamic_update_slice | solution.py:121
  715.0 6.0 copy.457
  724.3 7.9 multiply_reduce_fusion.2
  745.4 7.2 fusion.171
  752.7 15.0 reshape.1518
  768.9 4.6 fusion.130
  774.4 5.5 fusion.172
  780.9 43.4 %all-reduce.27 = (f32[8960]{0:T(1024)S(1)}, f32[3584]{0:T(1024)S(1)}, f32[3,24]{1,0:T(4,128)}) all-reduce(f32[8960]{0:T(1024)S(1)} %reshape.1519, f32[3584]{0:T(1024)S(1)} %pad_maximum_fusion.16, f32[3,24]{1,0:T(4,128)S(1)} %pad_add_fusion.2), channel_id=7, replica_groups=mesh['dp'=8,'ctx'=4] {'dp','ctx'}, use_global_device_ids=true, to_apply=%region_40.41.clone | all-reduce | flops 12616 | bytes 100928
  826.8 673.9 %all-reduce.32.cloned.1.call-done = (f32[3432448]{0:T(1024)}, f32[1572864]{0:T(1024)}, f32[786432]{0:T(1024)}, f32[524288]{0:T(1024)}, f32[4194304]{0:T(1024)}, /*index=5*/f32[2097152]{0:T(1024)}) async-done(((f32[3432448]{0:T(1024)}, f32[1572864]{0:T(1024)}, f32[786432]{0:T(1024)}, f32[524288]{0:T(1024)}, f32[4194304]{0:T(1024)}, /*index=5*/f32[2097152]{0:T(1024)}), (f32[3432448]{0:T(1024)}, ...) | async-done | bytes 50429968
  (559 shorter events, 269.0 us)
Async XLA Ops:
  7.2 6.6 copy-start.110
  7.2 7.2 copy-start.112
  7.2 7.4 copy-start.111
  7.2 109.4 %all-gather.26.cloned.1.call-start = ((), (), s32[]{:S(2)}) async-start(), calls=%async_computation.11 | async-start | bytes 14158848 | tf_op jit(solution)/shard_map/all_gather | solution.py:213
  9.2 319.3 %all-gather.16.cloned.1.call-start = ((), (), s32[]{:S(2)}) async-start(), calls=%async_computation.4 | async-start | bytes 1081344 | tf_op jit(solution)/shard_map/all_gather | solution.py:217
  9.9 320.8 %all-gather.14.cloned.1.call-start = ((), (), s32[]{:S(2)}) async-start(), calls=%async_computation.3 | async-start | bytes 1622016 | tf_op jit(solution)/shard_map/all_gather | solution.py:216
  10.7 355.2 %all-gather.12.cloned.1.call-start = ((), (), s32[]{:S(2)}) async-start(), calls=%async_computation.2 | async-start | bytes 3244032 | tf_op jit(solution)/shard_map/all_gather | solution.py:215
  11.3 360.5 %all-gather.20.cloned.1.call-start = ((), (), s32[]{:S(2)}) async-start(), calls=%async_computation.6 | async-start | bytes 4325376 | tf_op jit(solution)/shard_map/all_gather | solution.py:219
  11.8 399.1 %all-gather.22.cloned.1.call-start = ((), (), s32[]{:S(2)}) async-start(), calls=%async_computation.9 | async-start | bytes 1966080 | tf_op jit(solution)/shard_map/all_gather | solution.py:34
  13.7 221.7 %copy-start.88 = (f32[256]{0:T(256)}, f32[256]{0:T(256)S(1)}, u32[]{:S(2)}) copy-start(f32[256]{0:T(256)S(1)} %get-tuple-element.1115) | copy-start | bytes 3076
  14.3 229.0 %copy-start.101 = (f32[24]{0:T(128)}, f32[24]{0:T(128)S(1)}, u32[]{:S(2)}) copy-start(f32[24]{0:T(128)S(1)} %get-tuple-element.1108) | copy-start | bytes 292
  14.3 229.0 %copy-start.103 = (f32[24]{0:T(128)}, f32[24]{0:T(128)S(1)}, u32[]{:S(2)}) copy-start(f32[24]{0:T(128)S(1)} %get-tuple-element.1109) | copy-start | bytes 292
  57.8 58.8 %copy-start.95 = (bf16[3584]{0:T(1024)(128)(2,1)}, bf16[3584]{0:T(1024)(128)(2,1)S(1)}, u32[]{:S(2)}) copy-start(bf16[3584]{0:T(1024)(128)(2,1)S(1)} %get-tuple-element.1046) | copy-start | bytes 21508
  57.8 177.6 %copy-start.67 = (f32[1024]{0:T(1024)}, f32[1024]{0:T(1024)S(1)}, u32[]{:S(2)}) copy-start(f32[1024]{0:T(1024)S(1)} %get-tuple-element.1106) | copy-start | bytes 12292
  57.9 186.6 %copy-start.75 = (f32[1792]{0:T(1024)}, f32[1792]{0:T(1024)S(1)}, u32[]{:S(2)}) copy-start(f32[1792]{0:T(1024)S(1)} %get-tuple-element.1102) | copy-start | bytes 21508
  57.9 186.6 %copy-start.77 = (f32[1792]{0:T(1024)}, f32[1792]{0:T(1024)S(1)}, u32[]{:S(2)}) copy-start(f32[1792]{0:T(1024)S(1)} %get-tuple-element.1103) | copy-start | bytes 21508
  57.9 186.6 %copy-start.79 = (f32[1792]{0:T(1024)}, f32[1792]{0:T(1024)S(1)}, u32[]{:S(2)}) copy-start(f32[1792]{0:T(1024)S(1)} %get-tuple-element.1104) | copy-start | bytes 21508
  57.9 187.8 %copy-start.81 = (f32[1792]{0:T(1024)}, f32[1792]{0:T(1024)S(1)}, u32[]{:S(2)}) copy-start(f32[1792]{0:T(1024)S(1)} %get-tuple-element.1101) | copy-start | bytes 21508
  219.8 15.6 %copy-start.23 = (bf16[1,256,1024]{2,1,0:T(8,128)(2,1)S(1)}, bf16[1,256,1024]{2,1,0:T(8,128)(2,1)}, u32[]{:S(2)}) copy-start(bf16[1,256,1024]{2,1,0:T(8,128)(2,1)} %param.21) | copy-start | bytes 1572868
  240.7 3.5 collective-permute-start
  245.7 14.4 copy-start.14
  324.3 128.5 %all-gather.18.cloned.1.call-start = ((), (), s32[]{:S(2)}) async-start(), calls=%async_computation.5 | async-start | bytes 8650752 | tf_op jit(solution)/shard_map/all_gather | solution.py:218
  325.0 245.0 %reduce-scatter.3.cloned.1.call-start = ((), (), s32[]{:S(2)}) async-start(), calls=%async_computation.7 | async-start | bytes 327680 | tf_op jit(solution)/shard_map/reduce_scatter | solution.py:340
  342.9 15.3 %copy-start.45 = (pred[256,1024]{0,1:T(8,128)(4,1)S(1)}, pred[256,1024]{0,1:T(8,128)(4,1)}, u32[]{:S(2)}) copy-start(pred[256,1024]{0,1:T(8,128)(4,1)} %iota_compare_fusion.2) | copy-start | bytes 786436
  350.9 8.7 copy-start.43
  431.2 7.6 copy-start.24
  431.2 7.6 copy-start.39
  466.4 9.5 slice-start.2
  498.4 73.5 %reduce-scatter.5.cloned.1.call-start = ((), (), s32[]{:S(2)}) async-start(), calls=%async_computation.8 | async-start | bytes 327680 | tf_op jit(solution)/shard_map/reduce_scatter | solution.py:343
  498.4 8.7 copy-start.42
  512.7 66.8 %all-gather.24.cloned.1.call-start = ((), (), s32[]{:S(2)}) async-start(), calls=%async_computation.10 | async-start | bytes 1966080 | tf_op jit(solution)/shard_map/all_gather | solution.py:53
  530.8 969.9 %all-reduce.32.cloned.1.call-start = ((), (), s32[]{:S(2)}) async-start(), calls=%async_computation.12 | async-start | bytes 100859904
  562.0 7.0 copy-start.6
  562.0 7.0 copy-start.44
  592.5 6.8 copy-start.29
  609.1 6.7 copy-start.36
  609.1 6.7 copy-start.61
  628.9 24.5 %copy-start.4 = (f32[2,1,128,24,64]{2,4,3,1,0:T(8,128)S(1)}, f32[2,1,128,24,64]{2,4,3,1,0:T(8,128)}, u32[]{:S(2)}) copy-start(f32[2,1,128,24,64]{2,4,3,1,0:T(8,128)} %copy-done.3) | copy-start | bytes 4718596 | tf_op jit(solution)/shard_map/transpose(jvp())/while
  630.1 23.3 %copy-start.19 = (f32[2,1,128,128]{3,2,1,0:T(8,128)S(1)}, f32[2,1,128,128]{3,2,1,0:T(8,128)}, u32[]{:S(2)}) copy-start(f32[2,1,128,128]{3,2,1,0:T(8,128)} %copy-done.18) | copy-start | bytes 393220 | tf_op jit(solution)/shard_map/transpose(jvp())/while
  654.0 6.8 copy-start.29
  670.6 6.7 copy-start.36
  670.6 6.7 copy-start.61
  690.4 24.5 %copy-start.4 = (f32[2,1,128,24,64]{2,4,3,1,0:T(8,128)S(1)}, f32[2,1,128,24,64]{2,4,3,1,0:T(8,128)}, u32[]{:S(2)}) copy-start(f32[2,1,128,24,64]{2,4,3,1,0:T(8,128)} %copy-done.3) | copy-start | bytes 4718596 | tf_op jit(solution)/shard_map/transpose(jvp())/while
  691.6 23.3 %copy-start.19 = (f32[2,1,128,128]{3,2,1,0:T(8,128)S(1)}, f32[2,1,128,128]{3,2,1,0:T(8,128)}, u32[]{:S(2)}) copy-start(f32[2,1,128,128]{3,2,1,0:T(8,128)} %copy-done.18) | copy-start | bytes 393220 | tf_op jit(solution)/shard_map/transpose(jvp())/while
  724.3 7.9 copy-start.82
  737.8 3.9 collective-permute-start.1
  780.0 45.6 %copy-start.37 = (f32[1,256,1024]{2,1,0:T(8,128)S(1)}, f32[1,256,1024]{2,1,0:T(8,128)}, u32[]{:S(2)}) copy-start(f32[1,256,1024]{2,1,0:T(8,128)} %get-tuple-element.1058) | copy-start | bytes 3145732
  780.0 45.6 %copy-start.106 = (f32[256]{0:T(256)S(1)}, f32[256]{0:T(256)}, u32[]{:S(2)}) copy-start(f32[256]{0:T(256)} %get-tuple-element.1114) | copy-start | bytes 3076
  (93 other events, 308.9 us)
Sparse Core Ops, SparseCore 0:
  11.6 105.0 all-gather.25
  119.5 51.7 all-gather.15
  174.2 53.8 all-gather.13
  230.9 57.8 all-gather.11
  291.4 60.8 all-gather.19
  354.3 18.1 all-gather.21
  375.4 77.3 all-gather.17
  498.5 18.5 reduce-scatter.2
  520.3 20.0 reduce-scatter.4
  542.4 19.6 all-gather.23
  767.8 732.8 all-reduce.31
where the time goes:
time: 1540 us; the launch traced here: 1520 us
  waiting for transfers between devices  747 us (49%)
  local copies, waits for them, and re-layouts  294 us (19%)
  other arithmetic  220 us (14%)
  matrix products  129 us (8%)
  blocking collectives  105 us (7%)
  between operations  15.6 us (1%)
    unnamed x12, waiting for transfers between devices  677 us
    all_gather x1, other arithmetic, local(): lax.all_gather(flat_shards[0], ('dp', 'ctx'), axis=0, tiled=True)  103 us
    unnamed x2, blocking collectives  86.4 us
    dynamic_update_slice x10, local copies, waits for them, and re-layouts, run_spans(): lax.scan(jax.checkpoint(span_step), state, (split(inputs), split(b_proj),...  81.2 us
    all_gather x1, waiting for transfers between devices, local(): lax.all_gather(flat_shards[0], ('dp', 'ctx'), axis=0, tiled=True)  58.8 us
    unnamed x232, local copies, waits for them, and re-layouts  44.3 us
  transfers between devices with their start and end apart: 13, of which 3 were waited for; matrix products, arithmetic and copies ran while one was open for 26% of the time, Pallas kernels for 0%

commit v1 on v0

v1 whole, which is shorter than its diff:
```python
import jax
import jax.numpy as jnp
from jax import lax
from jax.sharding import PartitionSpec as P

D = 1024
MHEADS = 24
MDIM = 64
STATE = 128
KCONV = 4
AHEADS = 8
KVHEADS = 2
ADIM = 64
FF = 2048
SPAN = 128
DINNER = 1536
CONV_CH = 1792
PROJ = 3352


EPSILON = 1e-05
ROPE_BASE = 10000.0


def passed_along(value, axis, steps):
    count = lax.axis_size(axis)
    leading, last = (max(0, -steps), min(count, count - steps))
    return lax.ppermute(value, axis, [(source, source + steps) for source in range(leading, last)])


def rms_scale(values):
    return lax.rsqrt(jnp.mean(values * values, -1, keepdims=True) + EPSILON)


def rms_back(values, scale, gain, grad):
    scaled = grad * gain
    values_grad = scale * scaled - values * scale**3 * jnp.mean(scaled * values, -1, keepdims=True)
    gain_grad = jnp.sum(grad * values * scale, axis=(0, 1))
    return (values_grad, gain_grad)


def rotate(values, positions):
    half = values.shape[-1] // 2
    freqs = ROPE_BASE ** (-(jnp.arange(half).astype(jnp.float32) * 2.0 / values.shape[-1]))
    angles = positions[:, None] * freqs[None, :]
    cosine = jnp.cos(angles)[:, None, :]
    sine = jnp.sin(angles)[:, None, :]
    first = values[..., :half]
    second = values[..., half:]
    return jnp.concatenate([first * cosine - second * sine, second * cosine + first * sine], -1)


def masked_scores(grouped, key_all, causal):
    raw_scores = jnp.einsum(
        "btkgd,bskd->bkgts", grouped, key_all, preferred_element_type=jnp.float32
    ) * ADIM ** (-0.5)
    return jnp.where(causal, raw_scores, -jnp.inf)


def project(left, right):
    return jnp.einsum("btd,df->btf", left, right, preferred_element_type=jnp.float32)


def project_back(left, right):
    return jnp.einsum("btf,df->btd", left, right, preferred_element_type=jnp.float32)


def outer_sum(left, right):
    return jnp.einsum("btd,btf->df", left, right, preferred_element_type=jnp.float32)


WIDE = 4224
STEP_AT = DINNER + CONV_CH + (AHEADS + 2 * KVHEADS) * ADIM
PROJ_AT = DINNER + CONV_CH
ALL = ("dp", "ctx")
HIGH = lax.Precision.HIGHEST


def gathered(shard):
    return lax.all_gather(shard, ALL, axis=0, tiled=True)


def scattered(value):
    return lax.psum_scatter(value, ALL, scatter_dimension=0, tiled=True)


def per_head(values):
    return jnp.transpose(values.reshape(values.shape[0], MHEADS, MDIM), (1, 0, 2))


def flat_heads(values):
    return jnp.transpose(values, (1, 0, 2)).reshape(values.shape[1], DINNER)


def spread(per_step):
    return jnp.repeat(per_step, MDIM, axis=1)


def headed(left, right):
    return lax.dot_general(
        left.astype(jnp.bfloat16),
        right.astype(jnp.bfloat16),
        (((2,), (1,)), ((0,), (0,))),
        preferred_element_type=jnp.float32,
    )


def headed_t(left, right):
    return lax.dot_general(
        left.astype(jnp.bfloat16),
        right.astype(jnp.bfloat16),
        (((1,), (1,)), ((0,), (0,))),
        preferred_element_type=jnp.float32,
    )


def times(left, right, dims):
    return lax.dot_general(
        left.astype(jnp.bfloat16),
        right.astype(jnp.bfloat16),
        (dims, ((), ())),
        preferred_element_type=jnp.float32,
    )


def pack_state(state, total):
    lead = total.astype(jnp.bfloat16)
    rest = (total - lead.astype(jnp.float32)).astype(jnp.bfloat16)
    extra = jnp.zeros((16, STATE), jnp.bfloat16)
    extra = extra.at[0, :MHEADS].set(lead).at[1, :MHEADS].set(rest)
    return jnp.concatenate([state.astype(jnp.bfloat16), extra], 0)


def totals_of(packed):
    parts = packed[:, DINNER : DINNER + 2, :MHEADS].astype(jnp.float32)
    return parts[:, 0] + parts[:, 1]


def head_sum(values):
    return jnp.sum(values.reshape(values.shape[0], MHEADS, MDIM), -1)


def local(
    tokens,
    cotangent,
    expander,
    convolver,
    contractor,
    projector,
    combiner,
    widener,
    narrower,
    norm_gains,
    head_rates,
):
    devices = lax.axis_size("dp") * lax.axis_size("ctx")
    ctx_count = lax.axis_size("ctx")
    here = lax.axis_index("ctx")
    batch, rows = (tokens.shape[0], tokens.shape[1])
    count = D // devices
    small = convolver.shape[0] + norm_gains.shape[0]
    small_cols = -(-small // count)
    small_at = STEP_AT + MHEADS
    small_all = jnp.pad(
        jnp.concatenate([convolver, norm_gains], 0), (0, small_cols * count - small)
    ).reshape(count, small_cols)
    expander_rows = expander.reshape(count, PROJ)
    shard_first = jnp.concatenate(
        [
            expander_rows[:, :PROJ_AT],
            projector.reshape(count, -1),
            expander_rows[:, PROJ_AT:],
            small_all,
            jnp.zeros((count, WIDE - small_at - small_cols), jnp.bfloat16),
        ],
        1,
    )
    w_first = gathered(shard_first)
    contract_rows, combine_rows, narrow_rows = (
        DINNER // devices,
        AHEADS * ADIM // devices,
        FF // devices,
    )
    shard_second = jnp.concatenate(
        [
            contractor.reshape(contract_rows, D),
            combiner.reshape(combine_rows, D),
            narrower.reshape(narrow_rows, D),
        ],
        0,
    )
    shard_second, w_first = lax.optimization_barrier((shard_second, w_first))
    w_second = gathered(shard_second[None])
    w_contract = w_second[:, :contract_rows].reshape(DINNER, D)
    w_combine = w_second[:, contract_rows : contract_rows + combine_rows].reshape(AHEADS * ADIM, D)
    w_narrow = w_second[:, contract_rows + combine_rows :].reshape(FF, D)
    shard_widen, w_second_done = lax.optimization_barrier((widener.reshape(count, 2 * FF), w_second[0, 0, 0]))
    w_widen = gathered(shard_widen)

    small_back = w_first[:, small_at : small_at + small_cols].reshape(devices, -1)
    conv_full = small_back[:, : convolver.shape[0]].reshape(KCONV + 1, CONV_CH).astype(jnp.float32)
    gains = small_back[:, convolver.shape[0] : small].reshape(-1).astype(jnp.float32)
    first_gain = gains[:D]
    second_gain = gains[D : 2 * D]
    mixer_gain = gains[2 * D :]
    groups = AHEADS // KVHEADS
    stream = tokens.astype(jnp.float32)
    first_scale = rms_scale(stream)
    normed = (stream * first_scale * first_gain).astype(jnp.bfloat16)
    expanded = project(normed, w_first)[0]
    gate_branch = expanded[:, :DINNER]
    conv_input = expanded[:, DINNER:PROJ_AT].astype(jnp.bfloat16)
    raw_step = expanded[:, STEP_AT:small_at]
    projected = expanded[None, :, PROJ_AT:STEP_AT]
    edge = passed_along(conv_input[rows - (KCONV - 1) :], "ctx", 1)
    extended = jnp.concatenate([edge, conv_input], 0).astype(jnp.float32)
    mixed = conv_full[KCONV]
    for offset in range(KCONV):
        mixed = mixed + conv_full[offset] * extended[offset : offset + rows]
    mixed_sig = jax.nn.sigmoid(mixed)
    conv_act = mixed * mixed_sig
    inputs = conv_act[:, :DINNER]
    b_proj = conv_act[:, DINNER : DINNER + STATE]
    c_proj = conv_act[:, DINNER + STATE :]
    step_size = jax.nn.softplus(raw_step + head_rates[0])
    rate = jnp.exp(head_rates[1])
    log_decay = -step_size * rate
    lower = jnp.arange(rows)[:, None] >= jnp.arange(rows)[None, :]
    lower_ones = lower.astype(jnp.float32)
    cumul = jnp.dot(lower_ones, log_decay, precision=HIGH)
    cumul_t = cumul.T
    total = cumul[-1]
    decays = jnp.exp(jnp.where(lower[None], cumul_t[:, :, None] - cumul_t[:, None, :], -jnp.inf))
    intersection = times(c_proj, b_proj, ((1,), (1,)))
    mixing = (intersection[None] * decays).astype(jnp.bfloat16)
    stepped = inputs * spread(step_size)
    stepped_low = stepped.astype(jnp.bfloat16)
    stepped_heads = per_head(stepped_low)
    within = flat_heads(headed(mixing, stepped_heads))
    tail = spread(jnp.exp(total[None] - cumul))
    local_state = times(stepped * tail, b_proj, ((0,), (0,)))
    all_states = lax.all_gather(pack_state(local_state, total), "ctx", axis=0)
    totals = totals_of(all_states)
    turn = jnp.arange(ctx_count)
    reach_before = (turn[None, :] < here) & (turn[None, :] > turn[:, None])
    before = jnp.exp(jnp.einsum("kj,jh->kh", reach_before.astype(jnp.float32), totals, precision=HIGH))
    before = jnp.where((turn < here)[:, None], before, 0.0)
    reach_after = (turn[None, :] > here) & (turn[None, :] < turn[:, None])
    after = jnp.exp(jnp.einsum("kj,jh->kh", reach_after.astype(jnp.float32), totals, precision=HIGH))
    after = jnp.where((turn > here)[:, None], after, 0.0)
    entering = jnp.sum(spread(before)[:, :, None] * all_states[:, :DINNER].astype(jnp.float32), 0)
    grown = spread(jnp.exp(cumul))
    scan_out = within + grown * times(c_proj, entering, ((1,), (1,)))
    skip = spread(head_rates[2][None])
    scanned = scan_out + skip * inputs
    gate_sig = jax.nn.sigmoid(gate_branch)
    gate_act = gate_branch * gate_sig
    gated = (scanned * gate_act)[None]
    gated_scale = rms_scale(gated)
    gated_norm = (gated * gated_scale * mixer_gain).astype(jnp.bfloat16)
    mixer_branch = project(gated_norm, w_contract)
    query_pos = here * rows + jnp.arange(rows)
    positions = query_pos.astype(jnp.float32)
    queries = rotate(
        projected[..., : AHEADS * ADIM].reshape(batch, rows, AHEADS, ADIM), positions
    ).astype(jnp.bfloat16)
    keys = rotate(
        projected[..., AHEADS * ADIM : (AHEADS + KVHEADS) * ADIM].reshape(
            batch, rows, KVHEADS, ADIM
        ),
        positions,
    ).astype(jnp.bfloat16)
    values = (
        projected[..., (AHEADS + KVHEADS) * ADIM :]
        .reshape(batch, rows, KVHEADS, ADIM)
        .astype(jnp.bfloat16)
    )
    both = jnp.concatenate(
        [keys.reshape(batch, rows, -1), values.reshape(batch, rows, -1)], -1
    )
    both_all = lax.all_gather(both, "ctx", axis=1, tiled=True)
    key_all = both_all[..., : KVHEADS * ADIM].reshape(batch, -1, KVHEADS, ADIM)
    value_all = both_all[..., KVHEADS * ADIM :].reshape(batch, -1, KVHEADS, ADIM)
    key_pos = jnp.arange(rows * ctx_count)
    causal = key_pos[None, :] <= query_pos[:, None]
    grouped = queries.reshape(batch, rows, KVHEADS, groups, ADIM)
    scores = masked_scores(grouped, key_all, causal)
    maxima = jnp.max(scores, -1, keepdims=True)
    expos = jnp.exp(scores - maxima)
    totals = jnp.sum(expos, -1, keepdims=True)
    log_total = maxima + jnp.log(totals)
    probs = (expos / totals).astype(jnp.bfloat16)
    attended = jnp.einsum("bkgts,bskd->btkgd", probs, value_all, preferred_element_type=jnp.float32)
    attended = attended.reshape(batch, rows, AHEADS * ADIM).astype(jnp.bfloat16)
    attention_branch = project(attended, w_combine)
    middle = stream + mixer_branch + attention_branch
    second_scale = rms_scale(middle)
    second = (middle * second_scale * second_gain).astype(jnp.bfloat16)
    widened = project(second, w_widen)
    gate_value = widened[..., :FF]
    up_value = widened[..., FF:]
    feed_sig = jax.nn.sigmoid(gate_value)
    activated = (gate_value * feed_sig * up_value).astype(jnp.bfloat16)
    layer_output = (middle + project(activated, w_narrow)).astype(jnp.bfloat16)
    outer_grad = cotangent.astype(jnp.float32)
    narrow_grad = outer_sum(activated, cotangent)
    act_grad = project_back(cotangent, w_narrow)
    gate_grad = act_grad * up_value * feed_sig * (1.0 + gate_value * (1.0 - feed_sig))
    up_grad = act_grad * gate_value * feed_sig
    widened_grad = jnp.concatenate([gate_grad, up_grad], -1).astype(jnp.bfloat16)
    widen_grad = outer_sum(second, widened_grad)
    widen_own = scattered(widen_grad.astype(jnp.bfloat16))
    second_grad = project_back(widened_grad, w_widen)
    middle_part, second_gain_grad = rms_back(middle, second_scale, second_gain, second_grad)
    middle_grad = outer_grad + middle_part
    branch_grad = middle_grad.astype(jnp.bfloat16)
    combine_grad = outer_sum(attended, branch_grad)
    attended_grad = project_back(branch_grad, w_combine).astype(jnp.bfloat16)
    attended_grad = attended_grad.reshape(batch, rows, KVHEADS, groups, ADIM)
    scores = masked_scores(grouped, key_all, causal)
    float_probs = jnp.exp(scores - log_total)
    value_part = jnp.einsum(
        "bkgts,btkgd->bskd",
        float_probs.astype(jnp.bfloat16),
        attended_grad,
        preferred_element_type=jnp.float32,
    )
    probs_grad = jnp.einsum(
        "btkgd,bskd->bkgts", attended_grad, value_all, preferred_element_type=jnp.float32
    )
    centre = jnp.sum(probs_grad * float_probs, -1, keepdims=True)
    scores_grad = (float_probs * (probs_grad - centre)).astype(jnp.bfloat16)
    query_grad = ADIM ** (-0.5) * jnp.einsum(
        "bkgts,bskd->btkgd", scores_grad, key_all, preferred_element_type=jnp.float32
    )
    key_part = ADIM ** (-0.5) * jnp.einsum(
        "bkgts,btkgd->bskd", scores_grad, grouped, preferred_element_type=jnp.float32
    )
    keys_span = rows * ctx_count
    parts = jnp.concatenate(
        [
            key_part.astype(jnp.bfloat16).reshape(keys_span, -1),
            value_part.astype(jnp.bfloat16).reshape(keys_span, -1),
        ],
        -1,
    )
    part_sum = lax.psum_scatter(parts, "ctx", scatter_dimension=0, tiled=True).astype(jnp.float32)
    key_sum = part_sum[:, : KVHEADS * ADIM].reshape(batch, rows, KVHEADS, ADIM)
    value_sum = part_sum[:, KVHEADS * ADIM :].reshape(batch, rows, KVHEADS, ADIM)
    query_grad = rotate(query_grad.reshape(batch, rows, AHEADS, ADIM), -positions)
    key_sum = rotate(key_sum, -positions)
    projected_grad = jnp.concatenate(
        [
            query_grad.reshape(batch, rows, AHEADS * ADIM),
            key_sum.reshape(batch, rows, KVHEADS * ADIM),
            value_sum.reshape(batch, rows, KVHEADS * ADIM),
        ],
        -1,
    ).astype(jnp.bfloat16)
    contract_grad = outer_sum(gated_norm, branch_grad)
    second_sum = jnp.concatenate(
        [
            contract_grad.astype(jnp.bfloat16).reshape(devices, contract_rows, D),
            combine_grad.astype(jnp.bfloat16).reshape(devices, combine_rows, D),
            narrow_grad.astype(jnp.bfloat16).reshape(devices, narrow_rows, D),
        ],
        1,
    )
    second_own = scattered(second_sum)[0].astype(jnp.float32)
    gated_norm_grad = project_back(branch_grad, w_contract)
    gated_grad, mixer_gain_grad = rms_back(gated, gated_scale, mixer_gain, gated_norm_grad)
    gated_grad = gated_grad[0]
    scanned_grad = gated_grad * gate_act
    gate_branch_grad = gated_grad * scanned * gate_sig * (1.0 + gate_branch * (1.0 - gate_sig))
    outgoing = times(grown * scanned_grad, c_proj, ((0,), (0,)))
    all_grads = lax.all_gather(outgoing.astype(jnp.bfloat16), "ctx", axis=0)
    leaving = jnp.sum(spread(after)[:, :, None] * all_grads.astype(jnp.float32), 0)
    scanned_low = scanned_grad.astype(jnp.bfloat16)
    scanned_heads = per_head(scanned_low)
    mixing_grad = lax.dot_general(
        scanned_heads,
        stepped_heads,
        (((2,), (2,)), ((0,), (0,))),
        preferred_element_type=jnp.float32,
    )
    crossing = jnp.sum(mixing_grad * decays, 0)
    from_leaving = tail * times(b_proj, leaving, ((1,), (1,)))
    within_back = flat_heads(headed_t(mixing, scanned_heads))
    stepped_grad = within_back + from_leaving
    c_grad = times(crossing, b_proj, ((1,), (0,))) + times(
        grown * scanned_grad, entering, ((1,), (0,))
    )
    b_grad = times(crossing, c_proj, ((0,), (0,))) + times(tail * stepped, leaving, ((1,), (0,)))
    rounded_grad = scanned_low.astype(jnp.float32)
    rounded_step = stepped_low.astype(jnp.float32)
    tail_part = head_sum(stepped * from_leaving)
    cumul_grad = (
        head_sum(rounded_grad * within + scanned_grad * (scan_out - within))
        - head_sum(rounded_step * within_back)
        - tail_part
    )
    total_grad = jnp.sum(tail_part, 0) + jnp.exp(total) * jnp.sum(
        (leaving * entering).reshape(MHEADS, -1), -1
    )
    log_grad = (
        lax.dot_general(lower_ones, cumul_grad, (((0,), (0,)), ((), ())), precision=HIGH)
        + total_grad[None]
    )
    step_grad = head_sum(stepped_grad * inputs) - log_grad * rate
    raw_grad = step_grad * jax.nn.sigmoid(raw_step + head_rates[0])
    rates_local = jnp.stack(
        [
            jnp.sum(raw_grad, 0),
            jnp.sum(log_grad * log_decay, 0),
            jnp.sum(head_sum(scanned_grad * inputs), 0),
        ],
        0,
    )
    inputs_grad = stepped_grad * spread(step_size) + skip * scanned_grad
    act_back = jnp.concatenate([inputs_grad, b_grad, c_grad], 1)
    mixed_grad = act_back * mixed_sig * (1.0 + mixed * (1.0 - mixed_sig))
    conv_grad = jnp.stack(
        [jnp.sum(mixed_grad * extended[k : k + rows], 0) for k in range(KCONV)]
        + [jnp.sum(mixed_grad, 0)],
        0,
    )
    spill = jnp.concatenate([jnp.zeros((KCONV - 1, CONV_CH), jnp.float32), mixed_grad[: KCONV - 1]], 0)
    lead = sum(conv_full[k] * spill[KCONV - 1 - k : 2 * (KCONV - 1) - k] for k in range(KCONV - 1))
    returned = passed_along(lead, "ctx", -1)
    padded = jnp.concatenate([mixed_grad, jnp.zeros((KCONV - 1, CONV_CH), jnp.float32)], 0)
    conv_input_grad = sum(
        conv_full[k] * padded[KCONV - 1 - k : KCONV - 1 - k + rows] for k in range(KCONV)
    )
    conv_input_grad = conv_input_grad + jnp.concatenate(
        [jnp.zeros((rows - (KCONV - 1), CONV_CH), jnp.float32), returned], 0
    )
    rates_total = lax.psum(rates_local, ALL)
    first_back = jnp.concatenate(
        [
            gate_branch_grad.astype(jnp.bfloat16),
            conv_input_grad.astype(jnp.bfloat16),
            projected_grad[0],
            raw_grad.astype(jnp.bfloat16),
            jnp.zeros((rows, WIDE - small_at), jnp.bfloat16),
        ],
        1,
    )[None]
    normed_grad = project_back(first_back, w_first)
    input_part, first_gain_grad = rms_back(stream, first_scale, first_gain, normed_grad)
    input_gradient = middle_grad + input_part
    gains_local = jnp.concatenate([first_gain_grad, second_gain_grad, mixer_gain_grad], 0)
    small_grads = jnp.concatenate(
        [conv_grad.reshape(devices, -1), gains_local.reshape(devices, -1)], 1
    )
    small_grads = jnp.pad(small_grads, ((0, 0), (0, small_cols * count - small))).reshape(
        D, small_cols
    )
    first_grad = outer_sum(normed, first_back)
    first_sum = jnp.concatenate(
        [
            first_grad[:, :STEP_AT],
            jnp.concatenate(
                [
                    first_grad[:, STEP_AT:small_at],
                    small_grads,
                    jnp.zeros((D, WIDE - small_at - small_cols), jnp.float32),
                ],
                1,
            ),
        ],
        1,
    ).astype(jnp.bfloat16)
    first_own = scattered(first_sum).astype(jnp.float32)
    small_own = first_own[:, small_at : small_at + small_cols].reshape(-1)
    return (
        layer_output,
        input_gradient,
        jnp.concatenate([first_own[:, :PROJ_AT], first_own[:, STEP_AT:small_at]], 1).reshape(-1),
        small_own[: convolver.shape[0]],
        second_own[:contract_rows].reshape(-1),
        first_own[:, PROJ_AT:STEP_AT].reshape(-1),
        second_own[contract_rows : contract_rows + combine_rows].reshape(-1),
        widen_own.astype(jnp.float32).reshape(-1),
        second_own[contract_rows + combine_rows :].reshape(-1),
        small_own[convolver.shape[0] : small],
        rates_total,
    )


def solution(mesh):
    return jax.shard_map(
        local,
        mesh=mesh,
        in_specs=(
            P("dp", "ctx", None),
            P("dp", "ctx", None),
            P(("dp", "ctx")),
            P(("dp", "ctx")),
            P(("dp", "ctx")),
            P(("dp", "ctx")),
            P(("dp", "ctx")),
            P(("dp", "ctx")),
            P(("dp", "ctx")),
            P(("dp", "ctx")),
            P(),
        ),
        out_specs=(
            P("dp", "ctx", None),
            P("dp", "ctx", None),
            P(("dp", "ctx")),
            P(("dp", "ctx")),
            P(("dp", "ctx")),
            P(("dp", "ctx")),
            P(("dp", "ctx")),
            P(("dp", "ctx")),
            P(("dp", "ctx")),
            P(("dp", "ctx")),
            P(),
        ),
        check_vma=False,
    )
```

time: 1540 us -> 964 us (0.63)
  waiting for transfers between devices: 747 us -> 551 us
  other arithmetic: 220 us -> 66 us
  local copies, waits for them, and re-layouts: 294 us -> 150 us
  blocking collectives: 105 us -> 52.7 us
    unnamed x12 -> x10, waiting for transfers between devices: 677 us -> 66.8 us
    reduce_scatter x2 -> x3, waiting for transfers between devices: 0.04 us -> 288 us  [the longest x2 288 us: scattered(): return lax.psum_scatter(value, ALL, scatter_dimension=0, tiled=True)]
    all_gather x8 -> x5, waiting for transfers between devices: 69.8 us -> 196 us  [the longest x3 196 us: gathered(): return lax.all_gather(shard, ALL, axis=0, tiled=True)]
    all_gather x1 -> x0, other arithmetic: 103 us -> none  [local(): lax.all_gather(flat_shards[0], ('dp', 'ctx'), axis=0, tiled=True)]
    unnamed x2 -> x0, blocking collectives: 86.4 us -> none
    dynamic_update_slice x10 -> x0, local copies, waits for them, and re-layouts: 81.2 us -> none  [run_spans(): lax.scan(jax.checkpoint(span_step), state, (split(inputs), split(b_proj),...]
    reshape x12 -> x23, local copies, waits for them, and re-layouts: 78.1 us -> 20.6 us  [the longest x2 4.62 us: flat_heads(): return jnp.transpose(values, (1, 0, 2)).reshape(values.shape[1], DINNER)]
    concatenate x0 -> x5, local copies, waits for them, and re-layouts: none -> 45.3 us  [the longest x1 37.2 us: local(): jnp.concatenate([first_grad[:, :STEP_AT], jnp.concatenate([first_grad[:,...]
  transfers between devices with their start and end apart: 13 -> 11, of which waited for: 3 -> 6; matrix products, arithmetic and copies ran while one was open for 26% -> 16% of each run, Pallas kernels for 0% -> 0%
where the time goes in v1:
time: 964 us; the launch traced here: 954 us
  waiting for transfers between devices  551 us (57%)
  local copies, waits for them, and re-layouts  150 us (16%)
  matrix products  115 us (12%)
  other arithmetic  66 us (7%)
  blocking collectives  52.7 us (5%)
  between operations  15.7 us (2%)
    reduce_scatter x2, waiting for transfers between devices, scattered(): return lax.psum_scatter(value, ALL, scatter_dimension=0, tiled=True)  288 us
    all_gather x3, waiting for transfers between devices, gathered(): return lax.all_gather(shard, ALL, axis=0, tiled=True)  196 us
    unnamed x10, waiting for transfers between devices  66.8 us
    psum x1, blocking collectives, local(): rates_total = lax.psum(rates_local, ALL)  41.5 us
    concatenate x1, local copies, waits for them, and re-layouts, local(): jnp.concatenate([first_grad[:, :STEP_AT], jnp.concatenate([first_grad[:,...  37.2 us
    unnamed x224, local copies, waits for them, and re-layouts  27.1 us
    dot_general x5, matrix products, project(): jnp.einsum('btd,df->btf', left, right, preferred_element_type=jnp.float32)  21.8 us
  transfers between devices with their start and end apart: 11, of which 6 were waited for; matrix products, arithmetic and copies ran while one was open for 16% of the time, Pallas kernels for 0%

profile of v1, /device:TPU:0, one launch (start us, length us, event | category | flops | bytes accessed | tf_op | source)
XLA Modules:
  0.0 953.9 jit_solution(605969011866621075)
XLA Ops:
  13.0 79.7 %all-gather.9.cloned.1.call-done = bf16[1024,4224]{1,0:T(8,128)(2,1)} async-done(((bf16[32,4224]{1,0:T(8,128)(2,1)}), bf16[1024,4224]{1,0:T(8,128)(2,1)}) %all-gather.9.cloned.1.call-update) | async-done | bytes 8650768 | tf_op jit(solution)/shard_map/all_gather | solution.py:80
  94.3 8.1 fusion.147
  115.1 2.4 fusion.141
  127.9 11.2 %all_gather.28 = bf16[1,1024,256]{2,1,0:T(8,128)(2,1)S(1)} all-gather(bf16[1,256,256]{2,1,0:T(8,128)(2,1)S(1)} %pad_maximum_fusion.12), channel_id=1, replica_groups=mesh['dp'=8,'ctx'=4] {'ctx'}, dimensions={1}, use_global_device_ids=true | all-gather | bytes 655360 | tf_op jit(solution)/shard_map/all_gather | solution.py:281
  145.5 2.5 fusion.146
  155.8 3.0 fusion.13
  163.8 2.7 multiply_reduce_fusion.1
  166.5 4.5 multiply_reduce_fusion.9
  171.7 51.5 %all-gather.15.cloned.1.call-done = bf16[4096,1024]{1,0:T(8,128)(2,1)} async-done(((bf16[128,1024]{1,0:T(8,128)(2,1)}), bf16[4096,1024]{1,0:T(8,128)(2,1)}) %all-gather.15.cloned.1.call-update) | async-done | bytes 8388624 | tf_op jit(solution)/shard_map/all_gather | solution.py:80
  224.5 2.6 slice.367
  227.1 6.0 slice.382
  236.9 65.1 %all-gather.11.cloned.1.call-done = bf16[1024,4096]{1,0:T(8,128)(2,1)} async-done(((bf16[32,4096]{1,0:T(8,128)(2,1)}), bf16[1024,4096]{1,0:T(8,128)(2,1)}) %all-gather.11.cloned.1.call-update) | async-done | bytes 8388624 | tf_op jit(solution)/shard_map/all_gather | solution.py:80
  301.9 6.2 convolution_bitcast_fusion
  308.2 3.2 fusion.63
  311.5 3.1 fusion.57
  316.8 3.0 multiply_reduce_fusion.7
  322.8 9.2 fusion
  332.1 5.5 fusion.38
  339.9 6.7 fusion.8
  352.6 6.0 multiply_reduce_fusion.6
  360.8 2.3 copy.214
  363.2 3.8 fusion.12
  367.0 3.0 copy.217
  370.0 2.3 convolution_convert_fusion.3
  372.4 3.1 convolution_multiply_fusion.2
  378.1 3.0 copy.233
  381.2 2.2 reduce_sum.292
  383.4 3.8 multiply_reduce_fusion
  395.9 2.3 fusion.14
  400.4 5.5 fusion.136
  415.4 3.2 copy.236
  422.4 2.3 reduce_sum.293
  425.4 2.2 fusion.133
  435.7 2.5 add_convert_fusion
  438.2 4.7 concatenate.130
  442.9 7.8 fusion.55
  450.8 5.9 fusion.79
  456.7 7.8 slice.514
  465.4 37.2 %concatenate.133 = bf16[1024,4224]{0,1:T(8,128)(2,1)} concatenate(bf16[1024,4120]{0,1:T(8,128)(2,1)} %slice.514, bf16[1024,13]{0,1:T(8,128)(2,1)S(1)} %copy.240, bf16[1024,91]{0,1:T(8,128)(2,1)S(1)} %broadcast_in_dim.140), dimensions={1} | concatenate | bytes 17301504 | tf_op jit(solution)/shard_map/concatenate | solution.py:459
  502.6 11.6 %copy.258 = bf16[1024,4224]{1,0:T(8,128)(2,1)} copy(bf16[1024,4224]{0,1:T(8,128)(2,1)} %concatenate.133) | data formatting | bytes 17301504
  518.5 4.0 pad_maximum_fusion
  524.1 7.1 convolution_convert_fusion
  532.1 4.9 fusion.33
  537.0 41.5 %psum.7 = f32[3,24]{1,0:T(4,128)} all-reduce(f32[3,24]{1,0:T(4,128)S(1)} %pad_maximum_fusion.16), channel_id=1, replica_groups=mesh['dp'=8,'ctx'=4] {'dp','ctx'}, use_global_device_ids=true, to_apply=%region_36.37 | all-reduce | flops 72 | bytes 576 | tf_op jit(solution)/shard_map/psum | solution.py:437
  578.5 2.5 fusion.52
  581.0 66.0 %reduce-scatter.13.cloned.1.call-done = bf16[32,4224]{1,0:T(8,128)(2,1)} async-done(((bf16[1024,4224]{1,0:T(8,128)(2,1)}), bf16[32,4224]{1,0:T(8,128)(2,1)}) %reduce-scatter.13.cloned.1.call-update) | async-done | bytes 270352
  654.3 142.8 %reduce-scatter.9.cloned.1.call-done = bf16[1,128,1024]{2,1,0:T(8,128)(2,1)} async-done(((bf16[32,128,1024]{2,1,0:T(8,128)(2,1)}), bf16[1,128,1024]{2,1,0:T(8,128)(2,1)}) %reduce-scatter.9.cloned.1.call-update) | async-done | bytes 262160 | tf_op jit(solution)/shard_map/reduce_scatter | solution.py:84
  799.5 144.8 %reduce-scatter.11.cloned.1.call-done = bf16[32,4096]{1,0:T(8,128)(2,1)} async-done(((bf16[1024,4096]{1,0:T(8,128)(2,1)}), bf16[32,4096]{1,0:T(8,128)(2,1)}) %reduce-scatter.11.cloned.1.call-update) | async-done | bytes 262160 | tf_op jit(solution)/shard_map/reduce_scatter | solution.py:84
  (408 shorter events, 125.7 us)
Async XLA Ops:
  7.2 5.8 copy-start.99
  7.2 85.5 %all-gather.9.cloned.1.call-start = ((), (), s32[]{:S(2)}) async-start(), calls=%async_computation.4 | async-start | bytes 8921088 | tf_op jit(solution)/shard_map/all_gather | solution.py:80
  11.3 149.2 %all-gather.13.cloned.1.call-start = ((), (), s32[]{:S(2)}) async-start(), calls=%async_computation.9 | async-start | bytes 1986560 | tf_op jit(solution)/shard_map/all_gather | solution.py:242
  13.0 89.5 %copy-start.85 = (f32[256]{0:T(256)}, f32[256]{0:T(256)S(1)}, u32[]{:S(2)}) copy-start(f32[256]{0:T(256)S(1)} %get-tuple-element.106) | copy-start | bytes 3076
  13.0 94.1 %copy-start.96 = (f32[24]{0:T(128)}, f32[24]{0:T(128)S(1)}, u32[]{:S(2)}) copy-start(f32[24]{0:T(128)S(1)} %get-tuple-element.99) | copy-start | bytes 292
  13.0 94.2 %copy-start.102 = (f32[24]{0:T(128)}, f32[24]{0:T(128)S(1)}, u32[]{:S(2)}) copy-start(f32[24]{0:T(128)S(1)} %get-tuple-element.100) | copy-start | bytes 292
  94.3 8.1 copy-start.80
  103.8 9.8 %collective-permute-start = (bf16[3,1792]{1,0:T(4,128)(2,1)S(1)}, bf16[3,1792]{1,0:T(4,128)(2,1)S(1)}, u32[]{:S(2)}, u32[]{:S(2)}) collective-permute-start(bf16[3,1792]{1,0:T(4,128)(2,1)S(1)} %slice.347), channel_id=1, source_target_pairs={{0,1},{1,2},{2,3},{4,5},{5,6},{6,7},{8,9},{9,10},{10,11},{12,13},{... | collective-permute-start | bytes 32264 | tf_op jit(solution)/shard_map/ppermute | solution.py:28
  108.9 6.1 copy-start.61
  108.9 6.1 copy-start.63
  108.9 6.1 copy-start.66
  109.0 6.1 copy-start.78
  121.4 101.8 %all-gather.15.cloned.1.call-start = ((), (), s32[]{:S(2)}) async-start(), calls=%async_computation.10 | async-start | bytes 8650752 | tf_op jit(solution)/shard_map/all_gather | solution.py:80
  122.1 179.8 %all-gather.11.cloned.1.call-start = ((), (), s32[]{:S(2)}) async-start(), calls=%async_computation.5 | async-start | bytes 8650752 | tf_op jit(solution)/shard_map/all_gather | solution.py:80
  123.0 268.0 %reduce-scatter.7.cloned.1.call-start = ((), (), s32[]{:S(2)}) async-start(), calls=%async_computation.6 | async-start | bytes 655360 | tf_op jit(solution)/shard_map/reduce_scatter | solution.py:347
  224.4 8.7 copy-start.25
  227.0 6.5 copy-start.5
  227.0 6.1 copy-start.51
  301.9 6.3 copy-start.37
  301.9 6.3 copy-start.41
  301.9 9.5 slice-start
  322.8 9.2 copy-start.39
  339.9 6.7 copy-start.44
  339.9 6.7 copy-start.46
  352.5 43.3 %all-gather.17.cloned.1.call-start = ((), (), s32[]{:S(2)}) async-start(), calls=%async_computation.11 | async-start | bytes 1966080 | tf_op jit(solution)/shard_map/all_gather | solution.py:376
  352.6 6.0 copy-start.12
  352.6 6.0 copy-start.15
  352.6 6.0 copy-start.16
  372.3 274.6 %reduce-scatter.13.cloned.1.call-start = ((), (), s32[]{:S(2)}) async-start(), calls=%async_computation.12 | async-start | bytes 8921088
  383.4 6.5 copy-start.23
  383.4 6.5 copy-start.33
  410.1 25.5 %collective-permute-start.1 = (f32[3,1792]{1,0:T(4,128)}, f32[3,1792]{1,0:T(4,128)}, u32[]{:S(2)}, u32[]{:S(2)}) collective-permute-start(f32[3,1792]{1,0:T(4,128)} %fusion.102), channel_id=1, source_target_pairs={{1,0},{2,1},{3,2},{5,4},{6,5},{7,6},{9,8},{10,9},{11,10},{13,12},{... | collective-permute-start | bytes 64520 | tf_op jit(solution)/shard_map/ppermute | solution.py:28
  420.7 12.2 %copy-start.90 = (bf16[1792]{0:T(1024)(128)(2,1)S(1)}, bf16[1792]{0:T(1024)(128)(2,1)}, u32[]{:S(2)}) copy-start(bf16[1792]{0:T(1024)(128)(2,1)} %get-tuple-element.39) | copy-start | bytes 10756
  420.7 12.8 %copy-start.89 = (bf16[1792]{0:T(1024)(128)(2,1)S(1)}, bf16[1792]{0:T(1024)(128)(2,1)}, u32[]{:S(2)}) copy-start(bf16[1792]{0:T(1024)(128)(2,1)} %get-tuple-element.47) | copy-start | bytes 10756
  422.4 13.3 %copy-start.29 = (f32[256,1792]{1,0:T(8,128)S(1)}, f32[256,1792]{1,0:T(8,128)}, u32[]{:S(2)}) copy-start(f32[256,1792]{1,0:T(8,128)} %copy-done.28) | copy-start | bytes 5505028
  422.4 13.3 %copy-start.65 = (f32[1792]{0:T(1024)S(1)}, f32[1792]{0:T(1024)}, u32[]{:S(2)}) copy-start(f32[1792]{0:T(1024)} %copy-done.63) | copy-start | bytes 21508
  422.4 13.3 %copy-start.68 = (f32[1792]{0:T(1024)S(1)}, f32[1792]{0:T(1024)}, u32[]{:S(2)}) copy-start(f32[1792]{0:T(1024)} %copy-done.66) | copy-start | bytes 21508
  422.4 13.3 %copy-start.79 = (f32[1792]{0:T(1024)S(1)}, f32[1792]{0:T(1024)}, u32[]{:S(2)}) copy-start(f32[1792]{0:T(1024)} %copy-done.78) | copy-start | bytes 21508
  424.7 13.5 %copy-start.56 = (bf16[256,128]{1,0:T(8,128)(2,1)S(1)}, bf16[256,128]{1,0:T(8,128)(2,1)}, u32[]{:S(2)}) copy-start(bf16[256,128]{1,0:T(8,128)(2,1)} %get-tuple-element.91) | copy-start | bytes 196612
  442.9 7.8 copy-start.27
  456.7 7.8 copy-start.91
  456.7 7.8 copy-start.98
  456.7 7.9 copy-start.73
  514.3 282.7 %reduce-scatter.9.cloned.1.call-start = ((), (), s32[]{:S(2)}) async-start(), calls=%async_computation.7 | async-start | bytes 8650752 | tf_op jit(solution)/shard_map/reduce_scatter | solution.py:84
  522.5 421.8 %reduce-scatter.11.cloned.1.call-start = ((), (), s32[]{:S(2)}) async-start(), calls=%async_computation.8 | async-start | bytes 8650752 | tf_op jit(solution)/shard_map/reduce_scatter | solution.py:84
  532.1 46.4 %copy-start.36 = (f32[1,256,1024]{2,1,0:T(8,128)S(1)}, f32[1,256,1024]{2,1,0:T(8,128)}, u32[]{:S(2)}) copy-start(f32[1,256,1024]{2,1,0:T(8,128)} %get-tuple-element.65) | copy-start | bytes 3145732
  532.1 46.4 %copy-start.93 = (f32[256]{0:T(256)S(1)}, f32[256]{0:T(256)}, u32[]{:S(2)}) copy-start(f32[256]{0:T(256)} %get-tuple-element.105) | copy-start | bytes 3076
  651.9 147.6 %copy-start.97 = (f32[416]{0:T(512)}, f32[416]{0:T(512)S(1)}, u32[]{:S(2)}) copy-start(f32[416]{0:T(512)S(1)} %reshape.792) | copy-start | bytes 4996
  (68 other events, 204.1 us)
Sparse Core Ops, SparseCore 0:
  11.5 81.1 all-gather.8
  121.5 21.2 all-gather.12
  145.7 77.3 all-gather.14
  225.9 76.0 all-gather.10
  352.7 20.2 reduce-scatter.6
  375.0 19.6 all-gather.16
  514.4 132.5 reduce-scatter.12
  649.4 147.6 reduce-scatter.8
  799.4 144.7 reduce-scatter.10

commit v2 on v1

--- a/solution.py
+++ b/solution.py
@@ -26,6 +26,15 @@
     count = lax.axis_size(axis)
     leading, last = (max(0, -steps), min(count, count - steps))
     return lax.ppermute(value, axis, [(source, source + steps) for source in range(leading, last)])
+
+
+def turned(value, steps):
+    count = lax.axis_size("ctx")
+    return lax.ppermute(value, "ctx", [(at, (at + steps) % count) for at in range(count)])
+
+
+def around(value):
+    return [value] + [turned(value, k) for k in range(1, lax.axis_size("ctx"))]
 
 
 def rms_scale(values):
@@ -239,9 +248,9 @@
     within = flat_heads(headed(mixing, stepped_heads))
     tail = spread(jnp.exp(total[None] - cumul))
     local_state = times(stepped * tail, b_proj, ((0,), (0,)))
-    all_states = lax.all_gather(pack_state(local_state, total), "ctx", axis=0)
+    all_states = jnp.stack(around(pack_state(local_state, total)), 0)
     totals = totals_of(all_states)
-    turn = jnp.arange(ctx_count)
+    turn = (here + ctx_count - jnp.arange(ctx_count)) % ctx_count
     reach_before = (turn[None, :] < here) & (turn[None, :] > turn[:, None])
     before = jnp.exp(jnp.einsum("kj,jh->kh", reach_before.astype(jnp.float32), totals, precision=HIGH))
     before = jnp.where((turn < here)[:, None], before, 0.0)
@@ -278,10 +287,11 @@
     both = jnp.concatenate(
         [keys.reshape(batch, rows, -1), values.reshape(batch, rows, -1)], -1
     )
-    both_all = lax.all_gather(both, "ctx", axis=1, tiled=True)
+    both_all = jnp.concatenate(around(both), 1)
     key_all = both_all[..., : KVHEADS * ADIM].reshape(batch, -1, KVHEADS, ADIM)
     value_all = both_all[..., KVHEADS * ADIM :].reshape(batch, -1, KVHEADS, ADIM)
-    key_pos = jnp.arange(rows * ctx_count)
+    sources = (here + ctx_count - jnp.arange(ctx_count)) % ctx_count
+    key_pos = (sources[:, None] * rows + jnp.arange(rows)[None, :]).reshape(-1)
     causal = key_pos[None, :] <= query_pos[:, None]
     grouped = queries.reshape(batch, rows, KVHEADS, groups, ADIM)
     scores = masked_scores(grouped, key_all, causal)
@@ -309,7 +319,10 @@
     up_grad = act_grad * gate_value * feed_sig
     widened_grad = jnp.concatenate([gate_grad, up_grad], -1).astype(jnp.bfloat16)
     widen_grad = outer_sum(second, widened_grad)
-    widen_own = scattered(widen_grad.astype(jnp.bfloat16))
+    widen_sum, widened_grad = lax.optimization_barrier(
+        (widen_grad.astype(jnp.bfloat16), widened_grad)
+    )
+    widen_own = scattered(widen_sum)
     second_grad = project_back(widened_grad, w_widen)
     middle_part, second_gain_grad = rms_back(middle, second_scale, second_gain, second_grad)
     middle_grad = outer_grad + middle_part
@@ -344,7 +357,9 @@
         ],
         -1,
     )
-    part_sum = lax.psum_scatter(parts, "ctx", scatter_dimension=0, tiled=True).astype(jnp.float32)
+    part_sum = parts[:rows].astype(jnp.float32)
+    for k in range(1, ctx_count):
+        part_sum = part_sum + turned(parts[k * rows : (k + 1) * rows], -k).astype(jnp.float32)
     key_sum = part_sum[:, : KVHEADS * ADIM].reshape(batch, rows, KVHEADS, ADIM)
     value_sum = part_sum[:, KVHEADS * ADIM :].reshape(batch, rows, KVHEADS, ADIM)
     query_grad = rotate(query_grad.reshape(batch, rows, AHEADS, ADIM), -positions)
@@ -366,14 +381,16 @@
         ],
         1,
     )
-    second_own = scattered(second_sum)[0].astype(jnp.float32)
+    second_sum, branch_grad = lax.optimization_barrier((second_sum, branch_grad))
+    second_sum, widen_own = lax.optimization_barrier((second_sum, widen_own))
+    second_own = scattered(second_sum)[0]
     gated_norm_grad = project_back(branch_grad, w_contract)
     gated_grad, mixer_gain_grad = rms_back(gated, gated_scale, mixer_gain, gated_norm_grad)
     gated_grad = gated_grad[0]
     scanned_grad = gated_grad * gate_act
     gate_branch_grad = gated_grad * scanned * gate_sig * (1.0 + gate_branch * (1.0 - gate_sig))
     outgoing = times(grown * scanned_grad, c_proj, ((0,), (0,)))
-    all_grads = lax.all_gather(outgoing.astype(jnp.bfloat16), "ctx", axis=0)
+    all_grads = jnp.stack(around(outgoing.astype(jnp.bfloat16)), 0)
     leaving = jnp.sum(spread(after)[:, :, None] * all_grads.astype(jnp.float32), 0)
     scanned_low = scanned_grad.astype(jnp.bfloat16)
     scanned_heads = per_head(scanned_low)
@@ -434,7 +451,6 @@
     conv_input_grad = conv_input_grad + jnp.concatenate(
         [jnp.zeros((rows - (KCONV - 1), CONV_CH), jnp.float32), returned], 0
     )
-    rates_total = lax.psum(rates_local, ALL)
     first_back = jnp.concatenate(
         [
             gate_branch_grad.astype(jnp.bfloat16),
@@ -456,20 +472,21 @@
         D, small_cols
     )
     first_grad = outer_sum(normed, first_back)
-    first_sum = jnp.concatenate(
-        [
-            first_grad[:, :STEP_AT],
-            jnp.concatenate(
-                [
-                    first_grad[:, STEP_AT:small_at],
-                    small_grads,
-                    jnp.zeros((D, WIDE - small_at - small_cols), jnp.float32),
-                ],
-                1,
-            ),
+    first_low = first_grad.astype(jnp.bfloat16)
+    last_columns = jnp.concatenate(
+        [
+            first_low[:, STEP_AT:small_at],
+            small_grads.astype(jnp.bfloat16),
+            jnp.zeros((D, WIDE - small_at - small_cols), jnp.bfloat16),
         ],
         1,
-    ).astype(jnp.bfloat16)
+    )
+    first_sum = lax.dynamic_update_slice(first_low, last_columns, (0, STEP_AT))
+    first_sum, rates_local, second_own = lax.optimization_barrier(
+        (first_sum, rates_local, second_own)
+    )
+    second_own = second_own.astype(jnp.float32)
+    rates_total = lax.psum(rates_local, ALL)
     first_own = scattered(first_sum).astype(jnp.float32)
     small_own = first_own[:, small_at : small_at + small_cols].reshape(-1)
     return (

time: 964 us -> 728 us (0.76)
  waiting for transfers between devices: 551 us -> 395 us
  local copies, waits for them, and re-layouts: 150 us -> 82.1 us
  blocking collectives: 52.7 us -> 37.3 us
  starting transfers between devices: 4.11 us -> 14.2 us
    unnamed x10 -> x6, waiting for transfers between devices: 66.8 us -> 0.1 us
    reduce_scatter x2 -> x3, waiting for transfers between devices: 288 us -> 222 us  [scattered(): return lax.psum_scatter(value, ALL, scatter_dimension=0, tiled=True)]
    all_gather x3, waiting for transfers between devices: 196 us -> 155 us  [gathered(): return lax.all_gather(shard, ALL, axis=0, tiled=True)]
    concatenate x1, local copies, waits for them, and re-layouts: 37.2 us -> 0.6 us  [local(): jnp.concatenate([first_low[:, STEP_AT:small_at], small_grads.astype(jnp.b...]
    ppermute x0 -> x12, waiting for transfers between devices: none -> 17.9 us  [turned(): lax.ppermute(value, 'ctx', [(at, (at + steps) % count) for at in range(co...]
    all_gather x1 -> x0, blocking collectives: 11.2 us -> none  [local(): both_all = lax.all_gather(both, 'ctx', axis=1, tiled=True)]
    unnamed x224 -> x216, local copies, waits for them, and re-layouts: 27.1 us -> 16.4 us
  transfers between devices with their start and end apart: 11 -> 20, of which waited for: 6 -> 9; matrix products, arithmetic and copies ran while one was open for 16% -> 30% of each run, Pallas kernels for 0% -> 0%
where the time goes in v2:
time: 728 us; the launch traced here: 718 us
  waiting for transfers between devices  395 us (54%)
  matrix products  112 us (15%)
  local copies, waits for them, and re-layouts  82.1 us (11%)
  other arithmetic  61 us (8%)
  blocking collectives  37.3 us (5%)
  between operations  15.8 us (2%)
  starting transfers between devices  14.2 us (2%)
    reduce_scatter x3, waiting for transfers between devices, scattered(): return lax.psum_scatter(value, ALL, scatter_dimension=0, tiled=True)  222 us
    all_gather x3, waiting for transfers between devices, gathered(): return lax.all_gather(shard, ALL, axis=0, tiled=True)  155 us
    psum x1, blocking collectives, local(): rates_total = lax.psum(rates_local, ALL)  37.3 us
    dot_general x5, matrix products, project_back(): jnp.einsum('btf,df->btd', left, right, preferred_element_type=jnp.float32)  23.8 us
    dot_general x9, matrix products, times(): lax.dot_general(left.astype(jnp.bfloat16), right.astype(jnp.bfloat16), (d...  20.6 us
    dot_general x5, matrix products, project(): jnp.einsum('btd,df->btf', left, right, preferred_element_type=jnp.float32)  19.4 us
    ppermute x12, waiting for transfers between devices, turned(): lax.ppermute(value, 'ctx', [(at, (at + steps) % count) for at in range(co...  17.9 us
    unnamed x216, local copies, waits for them, and re-layouts  16.4 us
  transfers between devices with their start and end apart: 20, of which 9 were waited for; matrix products, arithmetic and copies ran while one was open for 30% of the time, Pallas kernels for 0%

profile of v2, /device:TPU:0, one launch (start us, length us, event | category | flops | bytes accessed | tf_op | source)
XLA Modules:
  0.0 717.8 jit_solution(13786565495284147062)
XLA Ops:
  12.3 80.5 %all-gather.5.cloned.1.call-done = bf16[1024,4224]{1,0:T(8,128)(2,1)} async-done(((bf16[32,4224]{1,0:T(8,128)(2,1)}), bf16[1024,4224]{1,0:T(8,128)(2,1)}) %all-gather.5.cloned.1.call-update) | async-done | bytes 8650768 | tf_op jit(solution)/shard_map/all_gather | solution.py:89
  100.5 6.3 fusion.151
  112.4 4.0 collective-permute-start
  125.1 3.3 fusion.146
  135.3 4.1 fusion.13
  139.4 3.0 copy.187
  142.4 2.0 collective-permute-start.3
  151.9 2.1 copy-done
  154.1 2.2 fusion.45
  156.4 4.0 collective-permute-done.3
  162.0 2.8 multiply_reduce_fusion.2
  164.9 4.6 multiply_reduce_fusion.10
  170.1 9.2 %all-gather.9.cloned.1.call-done = bf16[4096,1024]{1,0:T(8,128)(2,1)} async-done(((bf16[128,1024]{1,0:T(8,128)(2,1)}), bf16[4096,1024]{1,0:T(8,128)(2,1)}) %all-gather.9.cloned.1.call-update) | async-done | bytes 8388624 | tf_op jit(solution)/shard_map/all_gather | solution.py:89
  180.6 2.6 slice.374
  183.2 6.0 slice.389
  190.3 2.1 multiply_reduce_fusion.11
  192.4 65.4 %all-gather.7.cloned.1.call-done = bf16[1024,4096]{1,0:T(8,128)(2,1)} async-done(((bf16[32,4096]{1,0:T(8,128)(2,1)}), bf16[1024,4096]{1,0:T(8,128)(2,1)}) %all-gather.7.cloned.1.call-update) | async-done | bytes 8388624 | tf_op jit(solution)/shard_map/all_gather | solution.py:89
  257.8 6.2 convolution_bitcast_fusion
  264.1 3.1 multiply_convert_fusion.4
  268.7 5.8 convolution_convert_fusion.1
  275.1 7.6 %fusion.60 = (bf16[1024]{0:T(1024)(128)(2,1)}, f32[256]{0:T(256)S(1)}, f32[256,1024]{1,0:T(8,128)S(1)}) fusion(f32[1,256,1024]{2,1,0:T(8,128)} %get-tuple-element.142, f32[256]{0:T(256)S(1)} %get-tuple-element.131, f32[1024]{0:T(1024)S(1)} %get-tuple-element.117, bf16[1024,4096]{1,0:T(8,128)(2,1)} %all-gather.7.cloned.1.call-done, ...), kind=kOutput, calls=%fused_computation.127 | convolution fusion | flops 2149055232 | bytes 12591104 | tf_op jit(solution)/shard_map/btf,df->btd/dot_general | solution.py:74
  287.0 4.0 pad_maximum_fusion
  291.0 131.2 %reduce-scatter.4.cloned.1.call-done = bf16[32,4096]{1,0:T(8,128)(2,1)} async-done(((bf16[1024,4096]{1,0:T(8,128)(2,1)}), bf16[32,4096]{1,0:T(8,128)(2,1)}) %reduce-scatter.4.cloned.1.call-update) | async-done | bytes 262160 | tf_op jit(solution)/shard_map/reduce_scatter | solution.py:93
  423.9 4.1 multiply_reduce_fusion.8
  428.1 4.1 multiply_reduce_fusion.7
  434.1 2.0 convolution_convert_fusion.4
  439.4 5.6 fusion.41
  446.8 3.1 copy.214
  449.9 2.2 reduce_sum.292
  453.9 3.9 fusion.12
  457.8 3.1 copy.198
  460.9 5.3 fusion
  466.2 4.6 fusion.8
  473.7 3.6 fusion.44
  480.3 3.5 multiply_reduce_fusion
  488.7 2.8 collective-permute-done.12
  493.1 11.1 %collective-permute-done.7 = bf16[1536,128]{1,0:T(8,128)(2,1)S(1)} collective-permute-done((bf16[1536,128]{1,0:T(8,128)(2,1)}, bf16[1536,128]{1,0:T(8,128)(2,1)S(1)}, u32[]{:S(2)}, u32[]{:S(2)}) %collective-permute-start.7) | collective-permute-done | bytes 393248 | tf_op jit(solution)/shard_map/ppermute | solution.py:33
  505.0 3.1 multiply_reduce_fusion.1
  511.0 6.9 fusion.141
  520.7 3.4 multiply_reduce_fusion.3
  531.9 2.2 reduce_sum.291
  544.4 3.9 concatenate.142
  548.3 7.8 %fusion.58 = (bf16[1024]{0:T(1024)(128)(2,1)S(1)}, f32[256]{0:T(256)S(1)}, f32[256,1024]{1,0:T(8,128)}) fusion(bf16[1,256,1024]{2,1,0:T(8,128)(2,1)S(1)} %copy-done.12, f32[256]{0:T(256)S(1)} %copy-done.80, f32[1024]{0:T(1024)S(1)} %get-tuple-element.118, bf16[256,4224]{1,0:T(8,128)(2,1)} %concatenate.142, bf16[1024,4224]{1,0:T(8,128)(2,1)} %all-gather.5.cloned.1.call-done), kind=kOutput, calls=%fused_computation.124 | convolution fusion | flops 2216426240 | bytes 12394496 | tf_op jit(solution)/shard_map/btf,df->btd/dot_general | solution.py:74
  557.0 7.6 %convolution_convert_fusion = bf16[1024,4224]{1,0:T(8,128)(2,1)} fusion(bf16[256,4224]{1,0:T(8,128)(2,1)} %concatenate.142, bf16[1,256,1024]{2,1,0:T(8,128)(2,1)S(1)} %copy-done.12, f32[1024]{0:T(1024)S(1)} %get-tuple-element.118, f32[256]{0:T(256)S(1)} %copy-done.80), kind=kOutput, calls=%fused_computation | convolution fusion | flops 2219966464 | bytes 11342848 | tf_op jit(solution)/shard_map/btd,btf->df/dot_general | solution.py:78
  566.5 3.0 reduce-scatter.6.cloned.1.call-done
  571.0 4.4 fusion.36
  579.9 37.3 %psum.7 = f32[3,24]{1,0:T(4,128)} all-reduce(f32[3,24]{1,0:T(4,128)S(1)} %copy-done.87), channel_id=1, replica_groups=mesh['dp'=8,'ctx'=4] {'dp','ctx'}, use_global_device_ids=true, to_apply=%region_35.36 | all-reduce | flops 72 | bytes 576 | tf_op jit(solution)/shard_map/psum | solution.py:489
  617.2 87.7 %reduce-scatter.8.cloned.1.call-done = bf16[32,4224]{1,0:T(8,128)(2,1)} async-done(((bf16[1024,4224]{1,0:T(8,128)(2,1)}), bf16[32,4224]{1,0:T(8,128)(2,1)}) %reduce-scatter.8.cloned.1.call-update) | async-done | bytes 270352 | tf_op jit(solution)/shard_map/reduce_scatter | solution.py:93
  (415 shorter events, 113.7 us)
Async XLA Ops:
  7.2 85.6 %copy-start.64 = (bf16[131072]{0:T(1024)(128)(2,1)S(1)}, bf16[131072]{0:T(1024)(128)(2,1)}, u32[]{:S(2)}) copy-start(bf16[131072]{0:T(1024)(128)(2,1)} %param.22) | copy-start | bytes 786436
  7.2 85.5 %all-gather.5.cloned.1.call-start = ((), (), s32[]{:S(2)}) async-start(), calls=%async_computation.3 | async-start | bytes 8921088 | tf_op jit(solution)/shard_map/all_gather | solution.py:89
  8.6 85.7 %copy-start.96 = (f32[3,24]{1,0:T(4,128)S(1)}, f32[3,24]{1,0:T(4,128)}, u32[]{:S(2)}) copy-start(f32[3,24]{1,0:T(4,128)} %param.25) | copy-start | bytes 868
  8.6 87.7 %copy-start.10 = (bf16[1,256,1024]{2,1,0:T(8,128)(2,1)S(1)}, bf16[1,256,1024]{2,1,0:T(8,128)(2,1)}, u32[]{:S(2)}) copy-start(bf16[1,256,1024]{2,1,0:T(8,128)(2,1)} %param.15) | copy-start | bytes 1572868
  11.3 168.0 %all-gather.9.cloned.1.call-start = ((), (), s32[]{:S(2)}) async-start(), calls=%async_computation.8 | async-start | bytes 8650752 | tf_op jit(solution)/shard_map/all_gather | solution.py:89
  92.7 165.1 %all-gather.7.cloned.1.call-start = ((), (), s32[]{:S(2)}) async-start(), calls=%async_computation.4 | async-start | bytes 8650752 | tf_op jit(solution)/shard_map/all_gather | solution.py:89
  93.6 328.6 %reduce-scatter.4.cloned.1.call-start = ((), (), s32[]{:S(2)}) async-start(), calls=%async_computation.5 | async-start | bytes 8650752 | tf_op jit(solution)/shard_map/reduce_scatter | solution.py:93
  94.3 22.1 %copy-start.91 = (f32[24]{0:T(128)}, f32[24]{0:T(128)S(1)}, u32[]{:S(2)}) copy-start(f32[24]{0:T(128)S(1)} %get-tuple-element.120) | copy-start | bytes 292
  94.3 22.3 %copy-start.97 = (f32[24]{0:T(128)}, f32[24]{0:T(128)S(1)}, u32[]{:S(2)}) copy-start(f32[24]{0:T(128)S(1)} %get-tuple-element.121) | copy-start | bytes 292
  97.1 9.7 %copy-start.79 = (f32[256]{0:T(256)}, f32[256]{0:T(256)S(1)}, u32[]{:S(2)}) copy-start(f32[256]{0:T(256)S(1)} %get-tuple-element.127) | copy-start | bytes 3076
  109.7 7.2 %copy-start.56 = (bf16[1,256,128]{2,1,0:T(8,128)(2,1)}, bf16[1,256,128]{2,1,0:T(8,128)(2,1)S(1)}, u32[]{:S(2)}) copy-start(bf16[1,256,128]{2,1,0:T(8,128)(2,1)S(1)} %copy.189) | copy-start | bytes 196612
  110.4 32.0 %collective-permute-start.6 = (bf16[1,256,256]{2,1,0:T(8,128)(2,1)}, bf16[1,256,256]{2,1,0:T(8,128)(2,1)}, u32[]{:S(2)}, u32[]{:S(2)}) collective-permute-start(bf16[1,256,256]{2,1,0:T(8,128)(2,1)} %pad_maximum_fusion.14), channel_id=1, source_target_pairs={{0,3},{1,0},{2,1},{3,2},{4,7},{5,4},{6,5},{7,6},{8,11},{9,8},{10,9... | collective-permute-start | bytes 393224 | tf_op jit(solution)/shard_map/ppermute | solution.py:33
  111.6 32.8 %collective-permute-start.5 = (bf16[1,256,256]{2,1,0:T(8,128)(2,1)}, bf16[1,256,256]{2,1,0:T(8,128)(2,1)}, u32[]{:S(2)}, u32[]{:S(2)}) collective-permute-start(bf16[1,256,256]{2,1,0:T(8,128)(2,1)} %pad_maximum_fusion.14), channel_id=1, source_target_pairs={{0,2},{1,3},{2,0},{3,1},{4,6},{5,7},{6,4},{7,5},{8,10},{9,11},{10,... | collective-permute-start | bytes 393224 | tf_op jit(solution)/shard_map/ppermute | solution.py:33
  112.3 32.2 %collective-permute-start.4 = (bf16[1,256,256]{2,1,0:T(8,128)(2,1)}, bf16[1,256,256]{2,1,0:T(8,128)(2,1)}, u32[]{:S(2)}, u32[]{:S(2)}) collective-permute-start(bf16[1,256,256]{2,1,0:T(8,128)(2,1)} %pad_maximum_fusion.14), channel_id=1, source_target_pairs={{0,1},{1,2},{2,3},{3,0},{4,5},{5,6},{6,7},{7,4},{8,9},{9,10},{10,1... | collective-permute-start | bytes 393224 | tf_op jit(solution)/shard_map/ppermute | solution.py:33
  112.4 11.3 %collective-permute-start = (bf16[3,1792]{1,0:T(4,128)(2,1)S(1)}, bf16[3,1792]{1,0:T(4,128)(2,1)}, u32[]{:S(2)}, u32[]{:S(2)}) collective-permute-start(bf16[3,1792]{1,0:T(4,128)(2,1)S(1)} %slice.356), channel_id=1, source_target_pairs={{0,1},{1,2},{2,3},{4,5},{5,6},{6,7},{8,9},{9,10},{10,11},{12,13},{... | collective-permute-start | bytes 32264 | tf_op jit(solution)/shard_map/ppermute | solution.py:28
  119.5 8.8 %copy-start.18 = (f32[256,1536]{1,0:T(8,128)}, f32[256,1536]{1,0:T(8,128)S(1)}, u32[]{:S(2)}) copy-start(f32[256,1536]{1,0:T(8,128)S(1)} %copy.185) | copy-start | bytes 4718596
  132.3 24.1 %collective-permute-start.2 = (bf16[1552,128]{1,0:T(8,128)(2,1)}, bf16[1552,128]{1,0:T(8,128)(2,1)S(1)}, u32[]{:S(2)}, u32[]{:S(2)}) collective-permute-start(bf16[1552,128]{1,0:T(8,128)(2,1)} %get-tuple-element.109), channel_id=1, source_target_pairs={{0,2},{1,3},{2,0},{3,1},{4,6},{5,7},{6,4},{7,5},{8,10},{9,11},{10,... | collective-permute-start | bytes 1191944 | tf_op jit(solution)/shard_map/ppermute | solution.py:33
  132.3 24.0 %collective-permute-start.1 = (bf16[1552,128]{1,0:T(8,128)(2,1)}, bf16[1552,128]{1,0:T(8,128)(2,1)}, u32[]{:S(2)}, u32[]{:S(2)}) collective-permute-start(bf16[1552,128]{1,0:T(8,128)(2,1)} %get-tuple-element.109), channel_id=1, source_target_pairs={{0,1},{1,2},{2,3},{3,0},{4,5},{5,6},{6,7},{7,4},{8,9},{9,10},{10,1... | collective-permute-start | bytes 1191944 | tf_op jit(solution)/shard_map/ppermute | solution.py:33
  142.4 6.9 copy-start.43
  142.4 6.9 copy-start.47
  142.4 6.9 copy-start.49
  142.4 18.0 %collective-permute-start.3 = (bf16[1552,128]{1,0:T(8,128)(2,1)}, bf16[1552,128]{1,0:T(8,128)(2,1)}, u32[]{:S(2)}, u32[]{:S(2)}) collective-permute-start(bf16[1552,128]{1,0:T(8,128)(2,1)} %get-tuple-element.109), channel_id=1, source_target_pairs={{0,3},{1,0},{2,1},{3,2},{4,7},{5,4},{6,5},{7,6},{8,11},{9,8},{10,9... | collective-permute-start | bytes 1191944 | tf_op jit(solution)/shard_map/ppermute | solution.py:33
  154.1 7.5 %copy-start.99 = (pred[4]{0:T(512)(128)(4,1)S(1)}, pred[4]{0:T(512)(128)(4,1)}, u32[]{:S(2)}) copy-start(pred[4]{0:T(512)(128)(4,1)} %get-tuple-element.149) | copy-start | bytes 16
  154.1 7.5 %copy-start.101 = (s32[4]{0:T(128)S(1)}, s32[4]{0:T(128)}, u32[]{:S(2)}) copy-start(s32[4]{0:T(128)} %get-tuple-element.152) | copy-start | bytes 52
  180.6 8.6 %copy-start.25 = (bf16[32,16,1024]{2,1,0:T(8,128)(2,1)}, bf16[32,16,1024]{2,1,0:T(8,128)(2,1)S(1)}, u32[]{:S(2)}) copy-start(bf16[32,16,1024]{2,1,0:T(8,128)(2,1)S(1)} %slice.385) | copy-start | bytes 3145732
  183.2 6.5 copy-start.5
  274.5 295.0 %reduce-scatter.6.cloned.1.call-start = ((), (), s32[]{:S(2)}) async-start(), calls=%async_computation.6 | async-start | bytes 8650752 | tf_op jit(solution)/shard_map/reduce_scatter | solution.py:93
  275.1 7.6 %copy-start.7 = (f32[1,256,1024]{2,1,0:T(8,128)S(1)}, f32[1,256,1024]{2,1,0:T(8,128)}, u32[]{:S(2)}) copy-start(f32[1,256,1024]{2,1,0:T(8,128)} %get-tuple-element.142) | copy-start | bytes 3145732
  275.1 7.6 %copy-start.46 = (bf16[1,256,1024]{2,1,0:T(8,128)(2,1)S(1)}, bf16[1,256,1024]{2,1,0:T(8,128)(2,1)}, u32[]{:S(2)}) copy-start(bf16[1,256,1024]{2,1,0:T(8,128)(2,1)} %param.16) | copy-start | bytes 1572868
  291.0 131.9 %copy-start.76 = (f32[2,4,256]{2,1,0:T(4,128)S(1)}, f32[2,4,256]{2,1,0:T(4,128)}, u32[]{:S(2)}) copy-start(f32[2,4,256]{2,1,0:T(4,128)} %copy-done.75) | copy-start | bytes 24580
  291.0 131.9 %copy-start.83 = (f32[2,4,256]{2,1,0:T(4,128)S(1)}, f32[2,4,256]{2,1,0:T(4,128)}, u32[]{:S(2)}) copy-start(f32[2,4,256]{2,1,0:T(4,128)} %copy-done.82) | copy-start | bytes 24580
  291.0 131.9 %copy-start.93 = (f32[4,1,24]{2,1,0:T(1,128)S(1)}, f32[4,1,24]{2,1,0:T(1,128)}, u32[]{:S(2)}) copy-start(f32[4,1,24]{2,1,0:T(1,128)} %copy-done.92) | copy-start | bytes 1156
  291.0 132.0 %copy-start.98 = (pred[4]{0:T(512)(128)(4,1)S(1)}, pred[4]{0:T(512)(128)(4,1)}, u32[]{:S(2)}) copy-start(pred[4]{0:T(512)(128)(4,1)} %get-tuple-element.148) | copy-start | bytes 16
  291.0 132.0 %copy-start.102 = (s32[4]{0:T(128)S(1)}, s32[4]{0:T(128)}, u32[]{:S(2)}) copy-start(s32[4]{0:T(128)} %get-tuple-element.152) | copy-start | bytes 52
  422.3 282.7 %reduce-scatter.8.cloned.1.call-start = ((), (), s32[]{:S(2)}) async-start(), calls=%async_computation.7 | async-start | bytes 8921088 | tf_op jit(solution)/shard_map/reduce_scatter | solution.py:93
  436.1 57.0 %collective-permute-start.9 = (bf16[1536,128]{1,0:T(8,128)(2,1)}, bf16[1536,128]{1,0:T(8,128)(2,1)}, u32[]{:S(2)}, u32[]{:S(2)}) collective-permute-start(bf16[1536,128]{1,0:T(8,128)(2,1)} %convolution_convert_fusion.4), channel_id=1, source_target_pairs={{0,3},{1,0},{2,1},{3,2},{4,7},{5,4},{6,5},{7,6},{8,11},{9,8},{10,9... | collective-permute-start | bytes 1179656 | tf_op jit(solution)/shard_map/ppermute | solution.py:33
  436.3 56.8 %collective-permute-start.8 = (bf16[1536,128]{1,0:T(8,128)(2,1)}, bf16[1536,128]{1,0:T(8,128)(2,1)}, u32[]{:S(2)}, u32[]{:S(2)}) collective-permute-start(bf16[1536,128]{1,0:T(8,128)(2,1)} %convolution_convert_fusion.4), channel_id=1, source_target_pairs={{0,2},{1,3},{2,0},{3,1},{4,6},{5,7},{6,4},{7,5},{8,10},{9,11},{10,... | collective-permute-start | bytes 1179656 | tf_op jit(solution)/shard_map/ppermute | solution.py:33
  477.6 9.9 %collective-permute-start.11 = (bf16[256,256]{1,0:T(8,128)(2,1)S(1)}, bf16[256,256]{1,0:T(8,128)(2,1)S(1)}, u32[]{:S(2)}, u32[]{:S(2)}) collective-permute-start(bf16[256,256]{1,0:T(8,128)(2,1)S(1)} %get-tuple-element.103), channel_id=1, source_target_pairs={{0,3},{1,0},{2,1},{3,2},{4,7},{5,4},{6,5},{7,6},{8,11},{9,8},{10,9... | collective-permute-start | bytes 393224 | tf_op jit(solution)/shard_map/ppermute | solution.py:33
  479.6 9.1 %collective-permute-start.13 = (bf16[256,256]{1,0:T(8,128)(2,1)S(1)}, bf16[256,256]{1,0:T(8,128)(2,1)S(1)}, u32[]{:S(2)}, u32[]{:S(2)}) collective-permute-start(bf16[256,256]{1,0:T(8,128)(2,1)S(1)} %get-tuple-element.104), channel_id=1, source_target_pairs={{0,1},{1,2},{2,3},{3,0},{4,5},{5,6},{6,7},{7,4},{8,9},{9,10},{10,1... | collective-permute-start | bytes 393224 | tf_op jit(solution)/shard_map/ppermute | solution.py:33
  479.6 11.9 %collective-permute-start.12 = (bf16[256,256]{1,0:T(8,128)(2,1)S(1)}, bf16[256,256]{1,0:T(8,128)(2,1)S(1)}, u32[]{:S(2)}, u32[]{:S(2)}) collective-permute-start(bf16[256,256]{1,0:T(8,128)(2,1)S(1)} %get-tuple-element.105), channel_id=1, source_target_pairs={{0,2},{1,3},{2,0},{3,1},{4,6},{5,7},{6,4},{7,5},{8,10},{9,11},{10,... | collective-permute-start | bytes 393224 | tf_op jit(solution)/shard_map/ppermute | solution.py:33
  487.6 16.6 %collective-permute-start.7 = (bf16[1536,128]{1,0:T(8,128)(2,1)}, bf16[1536,128]{1,0:T(8,128)(2,1)S(1)}, u32[]{:S(2)}, u32[]{:S(2)}) collective-permute-start(bf16[1536,128]{1,0:T(8,128)(2,1)} %convolution_convert_fusion.4), channel_id=1, source_target_pairs={{0,1},{1,2},{2,3},{3,0},{4,5},{5,6},{6,7},{7,4},{8,9},{9,10},{10,1... | collective-permute-start | bytes 1179656 | tf_op jit(solution)/shard_map/ppermute | solution.py:33
  526.0 16.7 %collective-permute-start.10 = (f32[3,1792]{1,0:T(4,128)}, f32[3,1792]{1,0:T(4,128)}, u32[]{:S(2)}, u32[]{:S(2)}) collective-permute-start(f32[3,1792]{1,0:T(4,128)} %fusion.105), channel_id=1, source_target_pairs={{1,0},{2,1},{3,2},{5,4},{6,5},{7,6},{9,8},{10,9},{11,10},{13,12},{... | collective-permute-start | bytes 64520 | tf_op jit(solution)/shard_map/ppermute | solution.py:28
  534.6 8.1 %copy-start.28 = (f32[256,1792]{1,0:T(8,128)S(1)}, f32[256,1792]{1,0:T(8,128)}, u32[]{:S(2)}) copy-start(f32[256,1792]{1,0:T(8,128)} %copy-done.27) | copy-start | bytes 5505028
  535.4 9.0 %copy-start.36 = (bf16[256,1536]{1,0:T(8,128)(2,1)S(1)}, bf16[256,1536]{1,0:T(8,128)(2,1)}, u32[]{:S(2)}) copy-start(bf16[256,1536]{1,0:T(8,128)(2,1)} %get-tuple-element.89) | copy-start | bytes 2359300
  548.3 7.9 %copy-start.86 = (bf16[1536]{0:T(1024)(128)(2,1)S(1)}, bf16[1536]{0:T(1024)(128)(2,1)}, u32[]{:S(2)}) copy-start(bf16[1536]{0:T(1024)(128)(2,1)} %get-tuple-element.61) | copy-start | bytes 9220
  548.3 7.9 %copy-start.95 = (bf16[1024]{0:T(1024)(128)(2,1)S(1)}, bf16[1024]{0:T(1024)(128)(2,1)}, u32[]{:S(2)}) copy-start(bf16[1024]{0:T(1024)(128)(2,1)} %get-tuple-element.63) | copy-start | bytes 6148
  548.3 7.9 %copy-start.73 = (bf16[32,280]{1,0:T(8,128)(2,1)S(1)}, bf16[32,280]{1,0:T(8,128)(2,1)}, u32[]{:S(2)}) copy-start(bf16[32,280]{1,0:T(8,128)(2,1)} %reshape.847) | copy-start | bytes 53764
  557.0 8.6 %copy-start.100 = (bf16[128]{0:T(256)(128)(2,1)S(1)}, bf16[128]{0:T(256)(128)(2,1)}, u32[]{:S(2)}) copy-start(bf16[128]{0:T(256)(128)(2,1)} %pad.29.clone) | copy-start | bytes 772
  (75 other events, 233.9 us)
Sparse Core Ops, SparseCore 0:
  11.5 81.1 all-gather.4
  95.6 83.6 all-gather.8
  182.2 75.6 all-gather.6
  274.7 147.5 reduce-scatter.3
  424.4 145.0 reduce-scatter.5
  575.3 129.6 reduce-scatter.7
